TPU v7x, 32 devices: a whole 2x2x4 slice. The times are simulated.
32 devices in a mesh: section: 4 (over y, core), dp: 8 (over z, x).
Axes of the slice: x: 2, y: 2, z: 4, core: 2. Of those that a mesh axis runs over, the one named last changes fastest.
Arguments:
- block_input: bfloat16 [2, 5120, 768], P(None, 'dp'), may hold values from -6 to 6
- out_cotangent: bfloat16 [2, 5120, 768], P(None, 'dp'), may hold values from -6 to 6
- segment_ids: int32 [2, 5120], P(None, 'dp'), may hold values from 0 to 2, as said below
- grid_row: int32 [2, 5120], P(None, 'dp'), may hold values from 0 to 23, as said below
- grid_col: int32 [2, 5120], P(None, 'dp'), may hold values from 0 to 23, as said below
- valid_slot: int32 [2, 5120], P(None, 'dp'), may hold values from 0 to 1, as said below
- in_master: float32 [4, 768, 3072], P('section', 'dp')
- out_master: float32 [4, 3072, 768], P('section', 'dp'), may hold values from -0.109375 to 0.109375
- in_moment: float32 [4, 768, 3072], P('section', 'dp'), may hold values from -320 to 320
- out_moment: float32 [4, 3072, 768], P('section', 'dp'), may hold values from -320 to 320
- in_average: float32 [4, 768, 3072], P('section', 'dp')
- out_average: float32 [4, 3072, 768], P('section', 'dp'), may hold values from -0.109375 to 0.109375
- small_master: float32 [4, 7, 768], P('section')
- small_moment: float32 [4, 7, 768], P('section'), may hold values from -640 to 640
- small_average: float32 [4, 7, 768], P('section')
Outputs:
- section_outputs: bfloat16 [4, 2, 5120, 768], P('section', None, 'dp')
- input_grads: bfloat16 [4, 2, 5120, 768], P('section', None, 'dp')
- in_moment_new: float32 [4, 768, 3072], P('section', 'dp')
- in_master_new: float32 [4, 768, 3072], P('section', 'dp')
- in_average_new: float32 [4, 768, 3072], P('section', 'dp')
- out_moment_new: float32 [4, 3072, 768], P('section', 'dp')
- out_master_new: float32 [4, 3072, 768], P('section', 'dp')
- out_average_new: float32 [4, 3072, 768], P('section', 'dp')
- small_moment_new: float32 [4, 7, 768], P('section')
- small_master_new: float32 [4, 7, 768], P('section')
- small_average_new: float32 [4, 7, 768], P('section')
- branch_bias_grads: float32 [4, 768], P('section')
Inputs may be any that keep to these rules, and one draw needn't show every extreme that they name: `segment_ids`: each packed sequence of 640 slots holds whole images of 14, 20 or 24 patches a side, one after another; segment ids number them 0, 1, 2, ... in order; padding slots come last and carry the last image's id. `grid_row`: the patch's row in its image, row-major order; 0 on padding. `grid_col`: the patch's column in its image; 0 on padding. `valid_slot`: every sequence holds at least one image.
All inputs are finite; a program needn't handle non-finite values.
Results may differ from a plain program's by a relative error of at most 0.015.
Values may be sent and summed in bfloat16 or wider, within the bound.
No kernel may reach another device: no remote copies, remote signals or barrier semaphores. Data moves between devices by JAX's collectives and lax.ppermute only.
A program may use at most 512 MiB of HBM per device.

v0:
```python
import math

import jax
import jax.numpy as jnp
from jax import lax
from jax.sharding import PartitionSpec as P

HD = 64
SEQ = 640


NORM_EPS = 1e-06
MOMENTUM = 0.9
DECAY = 0.0001
AVERAGE = 0.8
RATE = 0.03
MASKED = -1e30
SQRT_HALF = 0.7071067811865476
INV_ROOT_TAU = 0.3989422804014327


def shifted(value, axis, by):
    length = lax.axis_size(axis)
    pairs = [(i, i + by) for i in range(length) if 0 <= i + by < length]
    return lax.ppermute(value, axis, pairs)


def layer_norm(stream, norm_gain, norm_shift):
    row_mean = jnp.mean(stream, axis=-1, keepdims=True)
    centered = stream - row_mean
    spread = jnp.mean(centered * centered, axis=-1, keepdims=True)
    inverse = lax.rsqrt(spread + NORM_EPS)
    normed = centered * inverse
    return (normed * norm_gain + norm_shift, normed, inverse)


def norm_chain(grad_lowered, normed, inverse, norm_gain, arriving):
    grad_gain = jnp.sum(grad_lowered * normed, axis=0)
    grad_shift = jnp.sum(grad_lowered, axis=0)
    scaled = grad_lowered * norm_gain
    inner = (
        scaled
        - jnp.mean(scaled, axis=-1, keepdims=True)
        - normed * jnp.mean(scaled * normed, axis=-1, keepdims=True)
    )
    return (arriving.astype(jnp.float32) + inverse * inner, grad_gain, grad_shift)


def rotate(vectors, cosine, sine_part):
    half_width = vectors.shape[-1] // 2
    first_half = vectors[..., :half_width]
    second_half = vectors[..., half_width:]
    return jnp.concatenate(
        [
            first_half * cosine - second_half * sine_part,
            first_half * sine_part + second_half * cosine,
        ],
        axis=-1,
    )


def rotation(frequency_row, grid_row, grid_col, head_count):
    frequency = frequency_row.reshape(head_count, 2, HD // 2)
    angles = (
        grid_col.astype(jnp.float32)[:, None, None] * frequency[None, :, 0]
        + grid_row.astype(jnp.float32)[:, None, None] * frequency[None, :, 1]
    )
    return (jnp.cos(angles), jnp.sin(angles))


def by_sequence(function, arrays):
    row_count = arrays[0].shape[0]
    seq_count = row_count // SEQ
    shaped = tuple((member.reshape((seq_count, SEQ) + member.shape[1:]) for member in arrays))
    outcome = lax.map(function, shaped)
    return jax.tree.map(
        lambda part_out: part_out.reshape((row_count,) + part_out.shape[2:]), outcome
    )


def group_layout(feature_width):
    head_count = feature_width // HD
    per_group = min(4, head_count)
    return (head_count, per_group, per_group * HD)


def head_probs(q_group, k_group, allowed, score_scale):
    raw_scores = (
        jnp.einsum("qhd,khd->hqk", q_group, k_group, preferred_element_type=jnp.float32)
        * score_scale
    )
    masked_scores = jnp.where(allowed[None], raw_scores, MASKED)
    top_score = jnp.max(masked_scores, axis=-1, keepdims=True)
    exponent = jnp.exp(masked_scores - top_score)
    return exponent / jnp.sum(exponent, axis=-1, keepdims=True)


def attend_sequence(sequence_item):
    queries, keys_rot, values, segment_ids, valid_slot = sequence_item
    length, feature_width = queries.shape
    head_count, per_group, group_width = group_layout(feature_width)
    allowed = (segment_ids[:, None] == segment_ids[None, :]) & (valid_slot[None, :] > 0)
    score_scale = HD ** (-0.5)

    def take_group(source, offset):
        return lax.dynamic_slice_in_dim(source, offset, group_width, 1).reshape(
            length, per_group, HD
        )

    def one_group(group_index, mixture):
        offset = group_index * group_width
        attend_weights = head_probs(
            take_group(queries, offset), take_group(keys_rot, offset), allowed, score_scale
        ).astype(jnp.bfloat16)
        outcome = jnp.einsum(
            "hqk,khd->qhd",
            attend_weights,
            take_group(values, offset),
            preferred_element_type=jnp.float32,
        )
        return lax.dynamic_update_slice_in_dim(
            mixture, outcome.reshape(length, group_width), offset, 1
        )

    return lax.fori_loop(
        0, head_count // per_group, one_group, jnp.zeros((length, feature_width), jnp.float32)
    )


def attend_sequence_back(sequence_item):
    queries, keys_rot, values, upstream, segment_ids, valid_slot = sequence_item
    length, feature_width = queries.shape
    head_count, per_group, group_width = group_layout(feature_width)
    allowed = (segment_ids[:, None] == segment_ids[None, :]) & (valid_slot[None, :] > 0)
    score_scale = HD ** (-0.5)

    def take_group(source, offset):
        return lax.dynamic_slice_in_dim(source, offset, group_width, 1).reshape(
            length, per_group, HD
        )

    def one_group(group_index, carried):
        grad_query, grad_key, grad_value = carried
        offset = group_index * group_width
        q_group = take_group(queries, offset)
        k_group = take_group(keys_rot, offset)
        v_group = take_group(values, offset)
        up_group = take_group(upstream, offset)
        probs_full = head_probs(q_group, k_group, allowed, score_scale)
        probs_low = probs_full.astype(jnp.bfloat16)
        grad_probs = jnp.einsum(
            "qhd,khd->hqk", up_group, v_group, preferred_element_type=jnp.float32
        )
        grad_v = jnp.einsum("hqk,qhd->khd", probs_low, up_group, preferred_element_type=jnp.float32)
        grad_scores = (
            probs_full * (grad_probs - jnp.sum(probs_full * grad_probs, axis=-1, keepdims=True))
        ).astype(jnp.bfloat16)
        grad_q = (
            jnp.einsum("hqk,khd->qhd", grad_scores, k_group, preferred_element_type=jnp.float32)
            * score_scale
        )
        grad_k = (
            jnp.einsum("hqk,qhd->khd", grad_scores, q_group, preferred_element_type=jnp.float32)
            * score_scale
        )
        grad_query = lax.dynamic_update_slice_in_dim(
            grad_query, grad_q.reshape(length, group_width), offset, 1
        )
        grad_key = lax.dynamic_update_slice_in_dim(
            grad_key, grad_k.reshape(length, group_width), offset, 1
        )
        grad_value = lax.dynamic_update_slice_in_dim(
            grad_value, grad_v.reshape(length, group_width), offset, 1
        )
        return (grad_query, grad_key, grad_value)

    empty = jnp.zeros((length, feature_width), jnp.float32)
    return lax.fori_loop(0, head_count // per_group, one_group, (empty, empty, empty))


def attention_inputs(entering, weight_in, small_params, grid_row, grid_col):
    stream = entering.astype(jnp.float32)
    row_count, feature_width = stream.shape
    head_count = feature_width // HD
    normed_out, normed, inverse = layer_norm(stream, small_params[0], small_params[1])
    lowered = normed_out.astype(jnp.bfloat16)
    bias_rows = small_params[2:6].reshape(-1)
    projected = (
        jnp.dot(lowered, weight_in[:, : 3 * feature_width], preferred_element_type=jnp.float32)
        + bias_rows[: 3 * feature_width]
    )
    queries = projected[:, :feature_width].reshape(row_count, head_count, HD)
    keys_plain = projected[:, feature_width : 2 * feature_width].reshape(row_count, head_count, HD)
    values = projected[:, 2 * feature_width :].astype(jnp.bfloat16)
    cosine, sine_part = rotation(small_params[6], grid_row, grid_col, head_count)
    query_rot = rotate(queries, cosine, sine_part)
    key_rot = rotate(keys_plain, cosine, sine_part)
    return (
        stream,
        normed,
        inverse,
        lowered,
        bias_rows,
        query_rot,
        key_rot,
        values,
        cosine,
        sine_part,
    )


def attention_forward(
    entering, weight_in, weight_out, small_params, segment_ids, grid_row, grid_col, valid_slot
):
    stream, normed, inverse, lowered, bias_rows, query_rot, key_rot, values, cosine, sine_part = (
        attention_inputs(entering, weight_in, small_params, grid_row, grid_col)
    )
    row_count, feature_width = stream.shape
    q_low = query_rot.reshape(row_count, feature_width).astype(jnp.bfloat16)
    k_low = key_rot.reshape(row_count, feature_width).astype(jnp.bfloat16)
    mixture = by_sequence(attend_sequence, (q_low, k_low, values, segment_ids, valid_slot))
    branch = (
        jnp.dot(
            mixture.astype(jnp.bfloat16),
            weight_in[:, 3 * feature_width :],
            preferred_element_type=jnp.float32,
        )
        + bias_rows[3 * feature_width :]
    )
    return stream + branch


def attention_backward(
    entering,
    arriving,
    weight_in,
    weight_out,
    small_params,
    segment_ids,
    grid_row,
    grid_col,
    valid_slot,
):
    stream, normed, inverse, lowered, bias_rows, query_rot, key_rot, values, cosine, sine_part = (
        attention_inputs(entering, weight_in, small_params, grid_row, grid_col)
    )
    row_count, feature_width = stream.shape
    head_count = feature_width // HD
    half_width = HD // 2
    q_low = query_rot.reshape(row_count, feature_width).astype(jnp.bfloat16)
    k_low = key_rot.reshape(row_count, feature_width).astype(jnp.bfloat16)
    mixture_low = by_sequence(
        attend_sequence, (q_low, k_low, values, segment_ids, valid_slot)
    ).astype(jnp.bfloat16)
    grad_out_proj = jnp.einsum(
        "tk,tn->kn", mixture_low, arriving, preferred_element_type=jnp.float32
    )
    grad_out_bias = jnp.sum(arriving.astype(jnp.float32), axis=0)
    grad_mixture = jnp.einsum(
        "tn,kn->tk", arriving, weight_in[:, 3 * feature_width :], preferred_element_type=jnp.float32
    ).astype(jnp.bfloat16)
    grad_qrot, grad_krot, grad_values = by_sequence(
        attend_sequence_back, (q_low, k_low, values, grad_mixture, segment_ids, valid_slot)
    )

    def unrotate(grad_rot, rotated):
        grad_rot = grad_rot.reshape(row_count, head_count, HD)
        grad_first = grad_rot[..., :half_width]
        grad_second = grad_rot[..., half_width:]
        unturned = jnp.concatenate(
            [
                grad_first * cosine + grad_second * sine_part,
                grad_second * cosine - grad_first * sine_part,
            ],
            axis=-1,
        )
        grad_angle = (
            grad_second * rotated[..., :half_width] - grad_first * rotated[..., half_width:]
        )
        return (unturned.reshape(row_count, feature_width), grad_angle)

    grad_query, angle_query = unrotate(grad_qrot, query_rot)
    grad_key, angle_key = unrotate(grad_krot, key_rot)
    grad_angle = angle_query + angle_key
    grad_freq_col = jnp.einsum(
        "thj,t->hj", grad_angle, grid_col.astype(jnp.float32), precision=lax.Precision.HIGHEST
    )
    grad_freq_row = jnp.einsum(
        "thj,t->hj", grad_angle, grid_row.astype(jnp.float32), precision=lax.Precision.HIGHEST
    )
    grad_frequency = jnp.stack([grad_freq_col, grad_freq_row], axis=1).reshape(feature_width)
    grad_projected = jnp.concatenate([grad_query, grad_key, grad_values], axis=1).astype(
        jnp.bfloat16
    )
    grad_in_proj = jnp.einsum(
        "tk,tn->kn", lowered, grad_projected, preferred_element_type=jnp.float32
    )
    grad_in_bias = jnp.sum(grad_projected.astype(jnp.float32), axis=0)
    grad_lowered = jnp.einsum(
        "tn,kn->tk",
        grad_projected,
        weight_in[:, : 3 * feature_width],
        preferred_element_type=jnp.float32,
    )
    grad_stream, grad_gain, grad_shift = norm_chain(
        grad_lowered, normed, inverse, small_params[0], arriving
    )
    grad_weight_in = jnp.concatenate([grad_in_proj, grad_out_proj], axis=1)
    bias_grads = jnp.concatenate([grad_in_bias, grad_out_bias]).reshape(4, feature_width)
    grad_small = jnp.concatenate(
        [grad_gain[None], grad_shift[None], bias_grads, grad_frequency[None]], axis=0
    )
    return (grad_stream, grad_weight_in, jnp.zeros(weight_out.shape, jnp.float32), grad_small)


def mlp_inputs(entering, weight_in, small_params):
    stream = entering.astype(jnp.float32)
    normed_out, normed, inverse = layer_norm(stream, small_params[0], small_params[1])
    lowered = normed_out.astype(jnp.bfloat16)
    gate_pre = jnp.dot(lowered, weight_in, preferred_element_type=jnp.float32) + small_params[
        2:6
    ].reshape(-1)
    activation = jax.nn.gelu(gate_pre, approximate=False).astype(jnp.bfloat16)
    return (stream, normed, inverse, lowered, gate_pre, activation)


def mlp_forward(
    entering, weight_in, weight_out, small_params, segment_ids, grid_row, grid_col, valid_slot
):
    stream, normed, inverse, lowered, gate_pre, activation = mlp_inputs(
        entering, weight_in, small_params
    )
    return stream + (
        jnp.dot(activation, weight_out, preferred_element_type=jnp.float32) + small_params[6]
    )


def mlp_backward(
    entering,
    arriving,
    weight_in,
    weight_out,
    small_params,
    segment_ids,
    grid_row,
    grid_col,
    valid_slot,
):
    stream, normed, inverse, lowered, gate_pre, activation = mlp_inputs(
        entering, weight_in, small_params
    )
    feature_width = stream.shape[1]
    grad_down = jnp.einsum("tf,td->fd", activation, arriving, preferred_element_type=jnp.float32)
    grad_down_bias = jnp.sum(arriving.astype(jnp.float32), axis=0)
    grad_act = jnp.einsum("td,fd->tf", arriving, weight_out, preferred_element_type=jnp.float32)
    slope = (
        0.5 * (1.0 + lax.erf(gate_pre * SQRT_HALF))
        + gate_pre * jnp.exp(-0.5 * gate_pre * gate_pre) * INV_ROOT_TAU
    )
    grad_gate = (grad_act * slope).astype(jnp.bfloat16)
    grad_up = jnp.einsum("tk,tf->kf", lowered, grad_gate, preferred_element_type=jnp.float32)
    grad_up_bias = jnp.sum(grad_gate.astype(jnp.float32), axis=0)
    grad_lowered = jnp.einsum("tf,kf->tk", grad_gate, weight_in, preferred_element_type=jnp.float32)
    grad_stream, grad_gain, grad_shift = norm_chain(
        grad_lowered, normed, inverse, small_params[0], arriving
    )
    grad_small = jnp.concatenate(
        [
            grad_gain[None],
            grad_shift[None],
            grad_up_bias.reshape(4, feature_width),
            grad_down_bias[None],
        ],
        axis=0,
    )
    return (grad_stream, grad_up, grad_down, grad_small)


def spare_forward(
    entering, weight_in, weight_out, small_params, segment_ids, grid_row, grid_col, valid_slot
):
    return jnp.zeros(entering.shape, jnp.float32)


def spare_backward(
    entering,
    arriving,
    weight_in,
    weight_out,
    small_params,
    segment_ids,
    grid_row,
    grid_col,
    valid_slot,
):
    return (
        jnp.zeros(entering.shape, jnp.float32),
        jnp.zeros(weight_in.shape, jnp.float32),
        jnp.zeros(weight_out.shape, jnp.float32),
        jnp.zeros(small_params.shape, jnp.float32),
    )


def pick_micro(source, micro_slot):
    return lax.dynamic_index_in_dim(source, micro_slot, 0, keepdims=False)


def store_micro(buffer, value, micro_slot, active):
    previous = pick_micro(buffer, micro_slot)
    return lax.dynamic_update_index_in_dim(
        buffer, jnp.where(active, value, previous), micro_slot, 0
    )


def advance(master, moment, average, gradient, step_rate):
    gradient = gradient + DECAY * master
    moment = MOMENTUM * moment + gradient
    master = master - step_rate * (gradient + MOMENTUM * moment)
    average = AVERAGE * average + (1 - AVERAGE) * master
    return (moment, master, average)


def on_device(
    block_input,
    out_cotangent,
    segment_ids,
    grid_row,
    grid_col,
    valid_slot,
    in_master,
    out_master,
    in_moment,
    out_moment,
    in_average,
    out_average,
    small_master,
    small_moment,
    small_average,
):
    section_index = lax.axis_index("section")
    section_count = lax.axis_size("section")
    micro_count, row_count, feature_width = block_input.shape
    weight_in, weight_out = (
        lax.all_gather(in_master.astype(jnp.bfloat16), "dp", axis=1, tiled=True),
        lax.all_gather(out_master.astype(jnp.bfloat16), "dp", axis=1, tiled=True),
    )
    weight_in = weight_in[0]
    weight_out = weight_out[0]
    small_params = small_master[0]
    branch_kind = jnp.where(section_index % 2 == 0, 1, 2)
    tick_count = micro_count + section_count - 1
    incoming = jnp.zeros((row_count, feature_width), jnp.bfloat16)
    kept_inputs = jnp.zeros(block_input.shape, jnp.bfloat16)
    kept_outputs = jnp.zeros(block_input.shape, jnp.bfloat16)
    for tick_index in range(tick_count):
        micro_index = tick_index - section_index
        active = (micro_index >= 0) & (micro_index < micro_count)
        micro_slot = jnp.clip(micro_index, 0, micro_count - 1)
        layout = tuple(
            (
                pick_micro(member, micro_slot)
                for member in (segment_ids, grid_row, grid_col, valid_slot)
            )
        )
        entering = jnp.where(section_index == 0, pick_micro(block_input, micro_slot), incoming)
        chosen = jnp.where(active, branch_kind, 0)
        result = lax.switch(
            chosen,
            (spare_forward, attention_forward, mlp_forward),
            entering,
            weight_in,
            weight_out,
            small_params,
            *layout
        )
        leaving = result.astype(jnp.bfloat16)
        kept_inputs = store_micro(kept_inputs, entering, micro_slot, active)
        kept_outputs = store_micro(kept_outputs, leaving, micro_slot, active)
        incoming = shifted(leaving, "section", 1)
    grad_in_total = jnp.zeros(weight_in.shape, jnp.float32)
    grad_out_total = jnp.zeros(weight_out.shape, jnp.float32)
    grad_small_total = jnp.zeros(small_params.shape, jnp.float32)
    returning = jnp.zeros((row_count, feature_width), jnp.bfloat16)
    input_grads = jnp.zeros(block_input.shape, jnp.bfloat16)
    for tick_index in range(tick_count):
        micro_index = tick_index - (section_count - 1 - section_index)
        active = (micro_index >= 0) & (micro_index < micro_count)
        micro_slot = jnp.clip(micro_index, 0, micro_count - 1)
        layout = tuple(
            (
                pick_micro(member, micro_slot)
                for member in (segment_ids, grid_row, grid_col, valid_slot)
            )
        )
        masked_cotangent = (
            pick_micro(out_cotangent, micro_slot) * layout[3].astype(jnp.bfloat16)[:, None]
        )
        arriving = jnp.where(section_index == section_count - 1, masked_cotangent, returning)
        entering = pick_micro(kept_inputs, micro_slot)
        chosen = jnp.where(active, branch_kind, 0)
        grad_stream, grad_in_part, grad_out_part, grad_small_part = lax.switch(
            chosen,
            (spare_backward, attention_backward, mlp_backward),
            entering,
            arriving,
            weight_in,
            weight_out,
            small_params,
            *layout
        )
        sent = grad_stream.astype(jnp.bfloat16)
        input_grads = store_micro(input_grads, sent, micro_slot, active)
        grad_in_total = grad_in_total + grad_in_part
        grad_out_total = grad_out_total + grad_out_part
        grad_small_total = grad_small_total + grad_small_part
        returning = shifted(sent, "section", -1)
    in_rows = in_master.shape[1]
    out_rows = out_master.shape[1]
    summed_in, summed_out, summed_small = (
        lax.psum(grad_in_total.astype(jnp.bfloat16), "dp").astype(jnp.float32),
        lax.psum(grad_out_total.astype(jnp.bfloat16), "dp").astype(jnp.float32),
        lax.psum(grad_small_total.astype(jnp.bfloat16), "dp").astype(jnp.float32),
    )
    owner = lax.axis_index("dp")
    share_in = lax.dynamic_slice_in_dim(summed_in, owner * in_rows, in_rows, 0)
    share_out = lax.dynamic_slice_in_dim(summed_out, owner * out_rows, out_rows, 0)
    branch_bias = jnp.where(section_index % 2 == 0, summed_small[5], summed_small[6])
    step_rate = RATE / math.sqrt(lax.axis_size("dp") * micro_count * row_count)
    in_moment_new, in_master_new, in_average_new = advance(
        in_master[0], in_moment[0], in_average[0], share_in, step_rate
    )
    out_moment_new, out_master_new, out_average_new = advance(
        out_master[0], out_moment[0], out_average[0], share_out, step_rate
    )
    small_moment_new, small_master_new, small_average_new = advance(
        small_master[0], small_moment[0], small_average[0], summed_small, step_rate
    )
    return (
        kept_outputs[None],
        input_grads[None],
        in_moment_new[None],
        in_master_new[None],
        in_average_new[None],
        out_moment_new[None],
        out_master_new[None],
        out_average_new[None],
        small_moment_new[None],
        small_master_new[None],
        small_average_new[None],
        branch_bias[None],
    )


def solution(mesh):
    placed = (
        P(None, "dp", None),
        P(None, "dp", None),
        P(None, "dp"),
        P(None, "dp"),
        P(None, "dp"),
        P(None, "dp"),
        P("section", "dp", None),
        P("section", "dp", None),
        P("section", "dp", None),
        P("section", "dp", None),
        P("section", "dp", None),
        P("section", "dp", None),
        P("section", None, None),
        P("section", None, None),
        P("section", None, None),
    )
    return jax.shard_map(
        on_device,
        mesh=mesh,
        in_specs=placed,
        out_specs=(
            P("section", None, "dp", None),
            P("section", None, "dp", None),
            P("section", "dp", None),
            P("section", "dp", None),
            P("section", "dp", None),
            P("section", "dp", None),
            P("section", "dp", None),
            P("section", "dp", None),
            P("section", None, None),
            P("section", None, None),
            P("section", None, None),
            P("section", None),
        ),
        check_vma=False,
    )
```

profile of v0, /device:TPU:0, one launch (start us, length us, event | category | flops | bytes accessed | tf_op | source)
XLA Modules:
  0.0 1579.9 jit_solution(10480360309884226302)
XLA Ops:
  13.5 80.0 %all-gather.3.cloned.1.call-done = bf16[1,768,3072]{2,1,0:T(8,128)(2,1)} async-done(((bf16[1,96,3072]{2,1,0:T(8,128)(2,1)}), bf16[1,768,3072]{2,1,0:T(8,128)(2,1)}) %all-gather.3.cloned.1.call-update) | async-done | bytes 4718608 | tf_op jit(solution)/shard_map/all_gather | solution.py:444
  93.4 80.8 %all-gather.5.cloned.1.call-done = bf16[1,3072,768]{2,1,0:T(8,128)(2,1)} async-done(((bf16[1,384,768]{2,1,0:T(8,128)(2,1)}), bf16[1,3072,768]{2,1,0:T(8,128)(2,1)}) %all-gather.5.cloned.1.call-update) | async-done | bytes 4718608 | tf_op jit(solution)/shard_map/all_gather | solution.py:445
  174.3 76.9 %conditional.10 = (bf16[640,768]{1,0:T(8,128)(2,1)}) conditional(s32[]{:T(128)} %clamp.30, () %tuple.468, (bf16[640,768]{1,0:T(8,128)(2,1)S(1)}, f32[7,768]{1,0:T(8,128)S(1)}, bf16[768,3072]{1,0:T(8,128)(2,1)}, s32[2,640]{1,0:T(2,128)S(1)}, s32[]{:T(128)}, /*index=5*/s32[2,640]{1,0:T(2,128)S(1)}, s32[2,640]{1,0:T(2,128)S(1)}, ...), branch_computations={%region_0.1_spmd, %region_1.8_spmd, %region_8.11_spmd} | conditional | flops 6177423872 | bytes 67641400 | solution.py:467
  198.6 41.2 %while.420 = (s32[]{:T(128)}, bf16[640,768]{0,1:T(8,128)(2,1)}, bf16[640,768]{1,0:T(8,128)(2,1)}, bf16[640,768]{0,1:T(8,128)(2,1)}, bf16[640,768]{0,1:T(8,128)(2...) while((s32[]{:T(128)}, bf16[640,768]{0,1:T(8,128)(2,1)}, ...), condition=%wide.region_7.7_spmd.clone, body=%wide.region_4.6_spmd.clone.sunk | while | flops 430080640 | bytes 18537768 | solution.py:125
  256.7 76.9 %conditional.11 = (bf16[640,768]{1,0:T(8,128)(2,1)}) conditional(s32[]{:T(128)} %clamp.31, () %tuple.471, (bf16[640,768]{1,0:T(8,128)(2,1)S(1)}, f32[7,768]{1,0:T(8,128)S(1)}, bf16[768,3072]{1,0:T(8,128)(2,1)}, s32[2,640]{1,0:T(2,128)S(1)}, s32[]{:T(128)}, /*index=5*/s32[2,640]{1,0:T(2,128)S(1)}, s32[2,640]{1,0:T(2,128)S(1)}, ...), branch_computations={%region_11.12_spmd, %region_12.19_spmd, %region_19.22_spmd} | conditional | flops 6177423872 | bytes 67641400 | solution.py:467
  281.0 41.2 %while.421 = (s32[]{:T(128)}, bf16[640,768]{0,1:T(8,128)(2,1)}, bf16[640,768]{1,0:T(8,128)(2,1)}, bf16[640,768]{0,1:T(8,128)(2,1)}, bf16[640,768]{0,1:T(8,128)(2...) while((s32[]{:T(128)}, bf16[640,768]{0,1:T(8,128)(2,1)}, ...), condition=%wide.region_18.18_spmd.clone, body=%wide.region_15.17_spmd.clone.sunk | while | flops 430080640 | bytes 18537768 | solution.py:125
  349.4 20.9 %collective-permute-start.2 = (bf16[640,768]{1,0:T(8,128)(2,1)}, bf16[640,768]{1,0:T(8,128)(2,1)}, u32[]{:S(2)}, u32[]{:S(2)}) collective-permute-start(bf16[640,768]{1,0:T(8,128)(2,1)} %get-tuple-element.6077), channel_id=1, source_target_pairs={{0,8},{8,16},{16,24},{1,9},{9,17},{17,25},{2,10},{10,18},{18,26},{... | collective-permute-start | bytes 2949128 | tf_op jit(solution)/shard_map/ppermute | solution.py:25
  380.2 23.1 %collective-permute-start.3 = (bf16[640,768]{1,0:T(8,128)(2,1)}, bf16[640,768]{1,0:T(8,128)(2,1)S(1)}, u32[]{:S(2)}, u32[]{:S(2)}) collective-permute-start(bf16[640,768]{1,0:T(8,128)(2,1)} %get-tuple-element.6078), channel_id=1, source_target_pairs={{0,8},{8,16},{16,24},{1,9},{9,17},{17,25},{2,10},{10,18},{18,26},{... | collective-permute-start | bytes 2949128 | tf_op jit(solution)/shard_map/ppermute | solution.py:25
  411.6 15.8 conditional.15
  428.7 81.4 %collective-permute-done.4 = bf16[640,768]{1,0:T(8,128)(2,1)S(1)} collective-permute-done((bf16[640,768]{1,0:T(8,128)(2,1)}, bf16[640,768]{1,0:T(8,128)(2,1)S(1)}, u32[]{:S(2)}, u32[]{:S(2)}) %collective-permute-start.4) | collective-permute-done | bytes 983072 | tf_op jit(solution)/shard_map/ppermute | solution.py:25
  511.5 14.8 conditional.16
  527.7 15.0 collective-permute-done.5
  544.1 15.8 conditional.17
  561.2 270.5 %collective-permute-done.6 = bf16[640,768]{1,0:T(8,128)(2,1)S(1)} collective-permute-done((bf16[640,768]{1,0:T(8,128)(2,1)}, bf16[640,768]{1,0:T(8,128)(2,1)S(1)}, u32[]{:S(2)}, u32[]{:S(2)}) %collective-permute-start.6) | collective-permute-done | bytes 983072 | tf_op jit(solution)/shard_map/ppermute | solution.py:25
  833.1 203.3 %conditional.18 = (f32[768,3072]{1,0:T(8,128)}, f32[3072,768]{1,0:T(8,128)}, f32[7,768]{1,0:T(8,128)S(1)}, bf16[640,768]{1,0:T(8,128)(2,1)}) conditional(s32[]{:T(128)} %clamp.38, () %tuple.492, (bf16[640,768]{1,0:T(8,128)(2,1)}, f32[7,768]{1,0:T(8,128)}, bf16[768,3072]{1,0:T(8,128)(2,1)}, s32[2,640]{1,0:T(2,128)}, ...), branch_computations={%region_139.140_spmd, %region_140.0_spmd, %region_158.167_spmd} | conditional | flops 15274486784 | bytes 317126976 | solution.py:501
  868.3 67.3 %while.431 = (s32[]{:T(128)}, f32[640,768]{0,1:T(8,128)}, f32[640,768]{0,1:T(8,128)}, bf16[640,768]{0,1:T(8,128)(2,1)}, bf16[640,768]{0,1:T(8,128)(2,1)}, /*inde...) while((s32[]{:T(128)}, f32[640,768]{0,1:T(8,128)}, ...), condition=%wide.region_147.147_spmd.clone, body=%wide.region_143.146_spmd.clone.sunk | while | flops 1071020160 | bytes 89357720 | solution.py:178
  950.1 35.7 %while.432 = (s32[]{:T(128)}, bf16[640,768]{0,1:T(8,128)(2,1)}, bf16[640,768]{0,1:T(8,128)(2,1)}, bf16[640,768]{0,1:T(8,128)(2,1)}, bf16[640,768]{0,1:T(8,128)(2...) while((s32[]{:T(128)}, bf16[640,768]{0,1:T(8,128)(2,1)}, ...), condition=%wide.region_151.151_spmd.clone, body=%wide.region_148.150_spmd.clone.sunk | while | flops 430080640 | bytes 17882408 | solution.py:125
  1042.5 191.0 %conditional.19 = (f32[768,3072]{1,0:T(8,128)}, f32[3072,768]{1,0:T(8,128)}, f32[7,768]{1,0:T(8,128)}, bf16[640,768]{1,0:T(8,128)(2,1)}) conditional(s32[]{:T(128)} %clamp.39, () %tuple.495, (bf16[640,768]{1,0:T(8,128)(2,1)S(1)}, f32[7,768]{1,0:T(8,128)}, bf16[768,3072]{1,0:T(8,128)(2,1)}, s32[2,640]{1,0:T(2,128)}, ...), branch_computations={%region_167.168_spmd, %region_168.186_spmd, %region_186.195_spmd} | conditional | flops 15274486784 | bytes 349501952 | solution.py:501
  1073.6 62.2 %while.433 = (s32[]{:T(128)}, f32[640,768]{0,1:T(8,128)}, f32[640,768]{0,1:T(8,128)}, bf16[640,768]{0,1:T(8,128)(2,1)S(1)}, bf16[640,768]{0,1:T(8,128)(2,1)}, /*...) while((s32[]{:T(128)}, f32[640,768]{0,1:T(8,128)}, ...), condition=%wide.region_175.175_spmd.clone, body=%wide.region_171.174_spmd.clone.sunk | while | flops 1071020160 | bytes 94600608 | solution.py:178
  1150.4 37.2 %while.434 = (s32[]{:T(128)}, bf16[640,768]{0,1:T(8,128)(2,1)}, bf16[640,768]{0,1:T(8,128)(2,1)}, bf16[640,768]{0,1:T(8,128)(2,1)}, bf16[640,768]{0,1:T(8,128)(2...) while((s32[]{:T(128)}, bf16[640,768]{0,1:T(8,128)(2,1)}, ...), condition=%wide.region_179.179_spmd.clone, body=%wide.region_176.178_spmd.clone.sunk | while | flops 430080640 | bytes 25746784 | solution.py:125
  1233.4 17.8 %add_convert_fusion.20 = bf16[3072,768]{1,0:T(8,128)(2,1)} fusion(f32[3072,768]{1,0:T(8,128)} %get-tuple-element.3376, f32[3072,768]{1,0:T(8,128)} %get-tuple-element.3375, f32[3072,768]{1,0:T(8,128)} %get-tuple-element.3374, f32[3072,768]{1,0:T(8,128)} %get-tuple-element.3372, f32[3072,768]{1,0:T(8,128)} %get-tuple-element.3373), kind=kLoop, calls=%fused_computation.1685 | loop fusion | flops 11796480 | bytes 51904512 | tf_op jit(solution)/shard_map/convert_element_type | solution.py:521
  1251.2 18.3 %add_convert_fusion.21 = bf16[768,3072]{1,0:T(8,128)(2,1)} fusion(f32[768,3072]{1,0:T(8,128)} %get-tuple-element.3371, f32[768,3072]{1,0:T(8,128)} %get-tuple-element.3370, f32[768,3072]{1,0:T(8,128)} %get-tuple-element.3369, f32[768,3072]{1,0:T(8,128)} %get-tuple-element.3367, f32[768,3072]{1,0:T(8,128)} %get-tuple-element.3368), kind=kLoop, calls=%fused_computation.1686 | loop fusion | flops 11796480 | bytes 51904512 | tf_op jit(solution)/shard_map/convert_element_type | solution.py:520
  1285.8 37.1 %psum.23 = bf16[7,768]{1,0:T(8,128)(2,1)S(1)} all-reduce(bf16[7,768]{1,0:T(8,128)(2,1)S(1)} %add_convert_fusion.22), channel_id=1, replica_groups=mesh['section'=4,'dp'=8] {'dp'}, use_global_device_ids=true, to_apply=%region_197.198 | all-reduce | flops 5376 | bytes 21504 | tf_op jit(solution)/shard_map/psum | solution.py:522
  1328.5 237.2 %all-reduce.3.cloned.1.call-done = (bf16[768,3072]{1,0:T(8,128)(2,1)}, bf16[3072,768]{1,0:T(8,128)(2,1)}) async-done(((bf16[768,3072]{1,0:T(8,128)(2,1)}, bf16[3072,768]{1,0:T(8,128)(2,1)}), (bf16[768,3072]{1,0:T(8,128)(2,1)}, bf16[3072,768]{1,0:T(8,128)(2,1)})) %all-reduce.3.cloned.1.call-update) | async-done | bytes 9437200 | tf_op jit(solution)/shard_map/psum | solution.py:520
  (626 shorter events, 634.1 us)
Async XLA Ops:
  7.2 167.1 %copy-start.119 = (s32[2,640]{1,0:T(2,128)S(1)}, s32[2,640]{1,0:T(2,128)}, u32[]{:S(2)}) copy-start(s32[2,640]{1,0:T(2,128)} %param.79) | copy-start | bytes 15364
  7.2 167.1 %copy-start.127 = (s32[2,640]{1,0:T(2,128)S(1)}, s32[2,640]{1,0:T(2,128)}, u32[]{:S(2)}) copy-start(s32[2,640]{1,0:T(2,128)} %param.78) | copy-start | bytes 15364
  7.2 167.0 %copy-start.135 = (s32[2,640]{1,0:T(2,128)S(1)}, s32[2,640]{1,0:T(2,128)}, u32[]{:S(2)}) copy-start(s32[2,640]{1,0:T(2,128)} %param.77) | copy-start | bytes 15364
  7.2 167.0 %copy-start.138 = (s32[2,640]{1,0:T(2,128)S(1)}, s32[2,640]{1,0:T(2,128)}, u32[]{:S(2)}) copy-start(s32[2,640]{1,0:T(2,128)} %param.80) | copy-start | bytes 15364
  7.2 86.2 %all-gather.3.cloned.1.call-start = ((), (), s32[]{:S(2)}) async-start(), calls=%async_computation | async-start | bytes 5308416 | tf_op jit(solution)/shard_map/all_gather | solution.py:444
  9.5 164.8 %all-gather.5.cloned.1.call-start = ((), (), s32[]{:S(2)}) async-start(), calls=%async_computation.1 | async-start | bytes 5308416 | tf_op jit(solution)/shard_map/all_gather | solution.py:445
  11.7 1554.1 %all-reduce.3.cloned.1.call-start = ((), (), s32[]{:S(2)}) async-start(), calls=%async_computation.2 | async-start | bytes 18874368 | tf_op jit(solution)/shard_map/psum | solution.py:520
  11.8 399.8 %copy-start.48 = (f32[1,7,768]{2,1,0:T(8,128)}, f32[1,7,768]{2,1,0:T(8,128)S(1)}, u32[]{:S(2)}) copy-start(f32[1,7,768]{2,1,0:T(8,128)S(1)} %copy.349) | copy-start | bytes 64516
  251.2 3.8 collective-permute-start
  333.6 3.8 collective-permute-start.1
  349.4 22.5 %collective-permute-start.2 = (bf16[640,768]{1,0:T(8,128)(2,1)}, bf16[640,768]{1,0:T(8,128)(2,1)}, u32[]{:S(2)}, u32[]{:S(2)}) collective-permute-start(bf16[640,768]{1,0:T(8,128)(2,1)} %get-tuple-element.6077), channel_id=1, source_target_pairs={{0,8},{8,16},{16,24},{1,9},{9,17},{17,25},{2,10},{10,18},{18,26},{... | collective-permute-start | bytes 2949128 | tf_op jit(solution)/shard_map/ppermute | solution.py:25
  380.2 26.8 %collective-permute-start.3 = (bf16[640,768]{1,0:T(8,128)(2,1)}, bf16[640,768]{1,0:T(8,128)(2,1)S(1)}, u32[]{:S(2)}, u32[]{:S(2)}) collective-permute-start(bf16[640,768]{1,0:T(8,128)(2,1)} %get-tuple-element.6078), channel_id=1, source_target_pairs={{0,8},{8,16},{16,24},{1,9},{9,17},{17,25},{2,10},{10,18},{18,26},{... | collective-permute-start | bytes 2949128 | tf_op jit(solution)/shard_map/ppermute | solution.py:25
  411.6 99.9 %copy-start.183 = (s32[1,640]{1,0:T(1,128)S(1)}, s32[1,640]{1,0:T(1,128)}, u32[]{:S(2)}) copy-start(s32[1,640]{1,0:T(1,128)} %get-tuple-element.4591) | copy-start | bytes 7684
  427.4 82.7 %collective-permute-start.4 = (bf16[640,768]{1,0:T(8,128)(2,1)}, bf16[640,768]{1,0:T(8,128)(2,1)S(1)}, u32[]{:S(2)}, u32[]{:S(2)}) collective-permute-start(bf16[640,768]{1,0:T(8,128)(2,1)} %get-tuple-element.3362), channel_id=1, source_target_pairs={{8,0},{16,8},{24,16},{9,1},{17,9},{25,17},{10,2},{18,10},{26,18},{... | collective-permute-start | bytes 2949128 | tf_op jit(solution)/shard_map/ppermute | solution.py:25
  526.3 16.3 %collective-permute-start.5 = (bf16[640,768]{1,0:T(8,128)(2,1)}, bf16[640,768]{1,0:T(8,128)(2,1)S(1)}, u32[]{:S(2)}, u32[]{:S(2)}) collective-permute-start(bf16[640,768]{1,0:T(8,128)(2,1)} %get-tuple-element.3363), channel_id=1, source_target_pairs={{8,0},{16,8},{24,16},{9,1},{17,9},{25,17},{10,2},{18,10},{26,18},{... | collective-permute-start | bytes 2949128 | tf_op jit(solution)/shard_map/ppermute | solution.py:25
  544.0 287.6 %copy-start.185 = (bf16[640]{0:T(1024)(128)(2,1)S(1)}, bf16[640]{0:T(1024)(128)(2,1)}, u32[]{:S(2)}) copy-start(bf16[640]{0:T(1024)(128)(2,1)} %get-tuple-element.4594) | copy-start | bytes 3844
  544.0 289.0 %copy-start.181 = (s32[1,640]{1,0:T(1,128)S(1)}, s32[1,640]{1,0:T(1,128)}, u32[]{:S(2)}) copy-start(s32[1,640]{1,0:T(1,128)} %get-tuple-element.4595) | copy-start | bytes 7684
  559.9 271.8 %collective-permute-start.6 = (bf16[640,768]{1,0:T(8,128)(2,1)}, bf16[640,768]{1,0:T(8,128)(2,1)S(1)}, u32[]{:S(2)}, u32[]{:S(2)}) collective-permute-start(bf16[640,768]{1,0:T(8,128)(2,1)} %get-tuple-element.3364), channel_id=1, source_target_pairs={{8,0},{16,8},{24,16},{9,1},{17,9},{25,17},{10,2},{18,10},{26,18},{... | collective-permute-start | bytes 2949128 | tf_op jit(solution)/shard_map/ppermute | solution.py:25
  833.0 208.0 %copy-start.184 = (bf16[640]{0:T(1024)(128)(2,1)S(1)}, bf16[640]{0:T(1024)(128)(2,1)}, u32[]{:S(2)}) copy-start(bf16[640]{0:T(1024)(128)(2,1)} %get-tuple-element.4266) | copy-start | bytes 3844
  833.0 209.4 %copy-start.5 = (bf16[640,768]{1,0:T(8,128)(2,1)S(1)}, bf16[640,768]{1,0:T(8,128)(2,1)}, u32[]{:S(2)}) copy-start(bf16[640,768]{1,0:T(8,128)(2,1)} %get-tuple-element.4580) | copy-start | bytes 2949124
  833.0 209.4 %copy-start.180 = (s32[1,640]{1,0:T(1,128)S(1)}, s32[1,640]{1,0:T(1,128)}, u32[]{:S(2)}) copy-start(s32[1,640]{1,0:T(1,128)} %get-tuple-element.4267) | copy-start | bytes 7684
  1036.4 4.7 collective-permute-start.7
  1283.7 282.1 %copy-start.52 = (f32[1,96,3072]{2,1,0:T(8,128)S(1)}, f32[1,96,3072]{2,1,0:T(8,128)}, u32[]{:S(2)}) copy-start(f32[1,96,3072]{2,1,0:T(8,128)} %param.81) | copy-start | bytes 3538948
  1328.5 241.3 %copy-start.53 = (f32[1,384,768]{2,1,0:T(8,128)S(1)}, f32[1,384,768]{2,1,0:T(8,128)}, u32[]{:S(2)}) copy-start(f32[1,384,768]{2,1,0:T(8,128)} %param.82) | copy-start | bytes 3538948
  (102 other events, 1394.4 us)
Sparse Core Ops, SparseCore 0:
  10.8 82.5 all-gather.2
  96.2 78.0 all-gather.4
  1269.6 296.1 all-reduce.2
where the time goes:
time: 1590 us; the launch traced here: 1580 us
  waiting for transfers between devices  773 us (49%)
  matrix products  260 us (16%)
  local copies, waits for them, and re-layouts  186 us (12%)
  other arithmetic  185 us (12%)
  loops' own time  70.4 us (4%)
  starting transfers between devices  53.8 us (3%)
  blocking collectives  37.1 us (2%)
    ppermute x8, waiting for transfers between devices, shifted(): return lax.ppermute(value, axis, pairs)  375 us
    psum x1, waiting for transfers between devices, on_device(): lax.psum(grad_in_total.astype(jnp.bfloat16), 'dp').astype(jnp.float32)  237 us
    sub x18, matrix products, head_probs(): exponent = jnp.exp(masked_scores - top_score)  97.4 us
    all_gather x1, waiting for transfers between devices, on_device(): lax.all_gather(out_master.astype(jnp.bfloat16), 'dp', axis=1, tiled=True)  80.8 us
    all_gather x1, waiting for transfers between devices, on_device(): lax.all_gather(in_master.astype(jnp.bfloat16), 'dp', axis=1, tiled=True)  80 us
    ppermute x8, starting transfers between devices, shifted(): return lax.ppermute(value, axis, pairs)  53.7 us
    dynamic_slice x54, local copies, waits for them, and re-layouts, take_group(): lax.dynamic_slice_in_dim(source, offset, group_width, 1)  51.3 us
    another operation x26, local copies, waits for them, and re-layouts  50.9 us
  transfers between devices with their start and end apart: 11, of which 10 were waited for; matrix products, arithmetic and copies ran while one was open for 2% of the time, Pallas kernels for 0%

commit v1 on v0

v1 whole, which is shorter than its diff:
```python
import functools
import math

import jax
import jax.numpy as jnp
from jax import lax
from jax.experimental import pallas as pl
from jax.experimental.pallas import tpu as pltpu
from jax.sharding import PartitionSpec as P

F32 = jnp.float32
BF16 = jnp.bfloat16
HD = 64
NORM_EPS = 1e-06
SQRT_HALF = 0.7071067811865476
INV_ROOT_TAU = 0.3989422804014327
LOG2E = 1.4426950408889634
VMEM_LIMIT = 56 * 1024 * 1024


def dot(lhs, rhs):
    return jnp.dot(lhs, rhs, preferred_element_type=F32)


def dot_t(lhs, rhs):
    return lax.dot_general(lhs, rhs, (((1,), (1,)), ((), ())), preferred_element_type=F32)


def tdot(lhs, rhs):
    return lax.dot_general(lhs, rhs, (((0,), (0,)), ((), ())), preferred_element_type=F32)


def normalize(stream):
    mean = jnp.mean(stream, axis=-1, keepdims=True)
    centered = stream - mean
    inverse = lax.rsqrt(jnp.mean(centered * centered, axis=-1, keepdims=True) + NORM_EPS)
    return centered * inverse, inverse


def lane_index(width):
    return lax.broadcasted_iota(jnp.int32, (1, width), 1)


def swap_halves(value):
    width = value.shape[1]
    first = (lane_index(width) % HD) < HD // 2
    return jnp.where(
        first, pltpu.roll(value, width - HD // 2, 1), pltpu.roll(value, HD // 2, 1)
    )


def attn_fwd_kernel(
    save, x_ref, small_ref, wq_ref, wk_ref, wv_ref, wo_ref, cos_ref, sin_ref, qe_ref, ke_ref, bq_ref, bk_ref, bv_ref, y_ref, *rest
):
    if save:
        q_out, k_out, v_out, e_out, linv_out, o_out, u_s, acc = rest
    else:
        u_s, acc = rest
    step = pl.program_id(0)
    last = pl.num_programs(0) - 1

    @pl.when(step == 0)
    def _():
        stream = x_ref[...].astype(F32)
        normed, _ = normalize(stream)
        u_s[...] = (normed * small_ref[0:1] + small_ref[1:2]).astype(BF16)
        acc[...] = stream + small_ref[5:6]

    lowered = u_s[...]
    cosine, sine = cos_ref[...], sin_ref[...]

    def turn(value):
        return (value * cosine + swap_halves(value) * sine).astype(BF16)

    q = turn(dot(lowered, wq_ref[...]) + bq_ref[...])
    k = turn(dot(lowered, wk_ref[...]) + bk_ref[...])
    v = (dot(lowered, wv_ref[...]) + bv_ref[...]).astype(BF16)
    if save:
        q_out[...] = q
        k_out[...] = k
        v_out[...] = v
    low_lane = lane_index(2 * HD) < HD
    scale = HD ** (-0.5) * LOG2E
    qe, ke = qe_ref[...], ke_ref[...]
    for pair in range(q.shape[1] // (2 * HD)):
        lanes = slice(pair * 2 * HD, (pair + 1) * 2 * HD)
        qp, kp, vp = q[:, lanes], k[:, lanes], v[:, lanes]
        qcat = jnp.concatenate([qp, qe], axis=1)
        sums = []
        for half in range(2):
            mine = low_lane if half == 0 else jnp.logical_not(low_lane)
            kcat = jnp.concatenate([jnp.where(mine, kp, jnp.zeros_like(kp)), ke], axis=1)
            scores = dot_t(qcat, kcat)
            top = jnp.max(scores, axis=-1, keepdims=True)
            e = jnp.exp2((scores - top) * scale).astype(BF16)
            if save:
                e_out[pair * 2 + half] = e
            sums.append(dot(e, jnp.where(mine, vp, jnp.ones_like(vp))))
        value = jnp.where(low_lane, sums[0], sums[1])
        total = pltpu.roll(jnp.where(low_lane, sums[1], sums[0]), HD, 1)
        inverse = 1.0 / total
        o = value * inverse
        if save:
            linv_out[:, lanes] = inverse
            o_out[:, lanes] = o
        acc[...] += dot(o.astype(BF16), wo_ref[lanes, :])

    @pl.when(step == last)
    def _():
        y_ref[...] = acc[...].astype(BF16)


def attn_fwd(save, x, small, w, cos, sin, qe, ke):
    rows, width = x.shape
    group = 4 * HD
    steps = width // group
    whole = pl.BlockSpec((rows, width), lambda g: (0, 0))
    part = pl.BlockSpec((rows, group), lambda g: (0, g))
    enc = pl.BlockSpec((rows, 128), lambda g: (0, 0))

    def wcol(base):
        return pl.BlockSpec(
            (None, width, group), lambda g, base=base: (base // 2, 0, base % 2 * steps + g)
        )

    def bias(row):
        return pl.BlockSpec((1, group), lambda g, row=row: (0, row * steps + g))

    flat = small[2:6].reshape(1, 4 * width)
    heads = width // HD
    out_shape = [jax.ShapeDtypeStruct((rows, width), BF16)]
    out_specs = [whole]
    if save:
        out_shape += [jax.ShapeDtypeStruct((rows, width), BF16)] * 3
        out_shape += [jax.ShapeDtypeStruct((heads, rows, rows), BF16)]
        out_shape += [jax.ShapeDtypeStruct((rows, width), F32)] * 2
        out_specs += [part] * 3 + [pl.BlockSpec((4, rows, rows), lambda g: (g, 0, 0))] + [part] * 2
    return pl.pallas_call(
        functools.partial(attn_fwd_kernel, save),
        grid=(steps,),
        in_specs=[
            whole,
            pl.BlockSpec((7, width), lambda g: (0, 0)),
            wcol(0), wcol(1), wcol(2),
            pl.BlockSpec((None, group, width), lambda g: (1, g, 1)),
            part, part, enc, enc,
            bias(0), bias(1), bias(2),
        ],
        out_specs=out_specs,
        out_shape=out_shape,
        scratch_shapes=[pltpu.VMEM((rows, width), BF16), pltpu.VMEM((rows, width), F32)],
        compiler_params=pltpu.CompilerParams(vmem_limit_bytes=VMEM_LIMIT),
        cost_estimate=pl.CostEstimate(
            flops=2 * rows * width * 4 * width + 4 * 4 * rows * rows * width,
            bytes_accessed=8 * width * width + 4 * rows * width,
            transcendentals=heads * rows * rows,
        ),
        name="attn_fwd",
    )(x, small, w, w, w, w, cos, sin, qe, ke, flat, flat, flat)


def mlp_fwd_kernel(save, x_ref, small_ref, bias_ref, wi_ref, wo_ref, y_ref, *rest):
    if save:
        z_out, slope_out, u_s, acc = rest
    else:
        u_s, acc = rest
    step = pl.program_id(0)

    @pl.when(step == 0)
    def _():
        stream = x_ref[...].astype(F32)
        normed, _ = normalize(stream)
        u_s[...] = (normed * small_ref[0:1] + small_ref[1:2]).astype(BF16)
        acc[...] = stream + small_ref[6:7]

    a = dot(u_s[...], wi_ref[...]) + bias_ref[...]
    phi = 0.5 + 0.5 * lax.erf(a * SQRT_HALF)
    z = (a * phi).astype(BF16)
    if save:
        z_out[...] = z
        slope_out[...] = (phi + a * jnp.exp2(a * a * (-0.5 * LOG2E)) * INV_ROOT_TAU).astype(BF16)
    acc[...] += dot(z, wo_ref[...])

    @pl.when(step == pl.num_programs(0) - 1)
    def _():
        y_ref[...] = acc[...].astype(BF16)


def mlp_fwd(save, x, small, wi, wo, tile=512):
    rows, width = x.shape
    hidden = 2 * wi.shape[2]
    steps = hidden // tile
    whole = pl.BlockSpec((rows, width), lambda g: (0, 0))
    part = pl.BlockSpec((rows, tile), lambda g: (0, g))
    out_shape = [jax.ShapeDtypeStruct((rows, width), BF16)]
    out_specs = [whole]
    if save:
        out_shape += [jax.ShapeDtypeStruct((rows, hidden), BF16)] * 2
        out_specs += [part] * 2
    return pl.pallas_call(
        functools.partial(mlp_fwd_kernel, save),
        grid=(steps,),
        in_specs=[
            whole,
            pl.BlockSpec((7, width), lambda g: (0, 0)),
            pl.BlockSpec((1, tile), lambda g: (0, g)),
            pl.BlockSpec((None, width, tile), lambda g: (g // (steps // 2), 0, g % (steps // 2))),
            pl.BlockSpec((tile, width), lambda g: (g, 0)),
        ],
        out_specs=out_specs,
        out_shape=out_shape,
        scratch_shapes=[pltpu.VMEM((rows, width), BF16), pltpu.VMEM((rows, width), F32)],
        compiler_params=pltpu.CompilerParams(vmem_limit_bytes=VMEM_LIMIT),
        cost_estimate=pl.CostEstimate(
            flops=4 * rows * width * hidden,
            bytes_accessed=4 * width * hidden + 4 * rows * width,
            transcendentals=2 * rows * hidden,
        ),
        name="mlp_fwd",
    )(x, small, small[2:6].reshape(1, hidden), wi, wo)


def norm_back(full, x_ref, gy_ref, small_ref, du, gx_ref, rows_ref):
    normed, inverse = normalize(x_ref[...].astype(F32))
    scaled = du * small_ref[0:1]
    inner = (
        scaled
        - jnp.mean(scaled, axis=-1, keepdims=True)
        - normed * jnp.mean(scaled * normed, axis=-1, keepdims=True)
    )
    gy = gy_ref[...].astype(F32)
    gx_ref[...] = (gy + inverse * inner).astype(BF16)
    if full:
        rows_ref[0:1] = jnp.sum(du * normed, axis=0, keepdims=True)
        rows_ref[1:2] = jnp.sum(du, axis=0, keepdims=True)
        rows_ref[2:3] = jnp.sum(gy, axis=0, keepdims=True)


def mlp_bwd_kernel(full, x_ref, gy_ref, small_ref, wi_ref, wo_ref, z_ref, slope_ref, gx_ref, *rest):
    if full:
        rows_ref, bias_ref, dwi_ref, dwo_ref, du_s, ut_s = rest
    else:
        rows_ref = None
        (du_s,) = rest
    step = pl.program_id(0)

    @pl.when(step == 0)
    def _():
        du_s[...] = jnp.zeros_like(du_s)
        if full:
            normed, _ = normalize(x_ref[...].astype(F32))
            lowered = (normed * small_ref[0:1] + small_ref[1:2]).astype(BF16)
            ut_s[...] = lowered.T

    gy = gy_ref[...]
    dz = dot_t(gy, wo_ref[...])
    da = (dz * slope_ref[...].astype(F32)).astype(BF16)
    du_s[...] += dot_t(da, wi_ref[...])
    if full:
        bias_ref[...] = jnp.sum(da.astype(F32), axis=0, keepdims=True)
        dwi_ref[...] = dot(ut_s[...], da).astype(BF16)
        dwo_ref[...] = tdot(z_ref[...], gy).astype(BF16)

    @pl.when(step == pl.num_programs(0) - 1)
    def _():
        norm_back(full, x_ref, gy_ref, small_ref, du_s[...], gx_ref, rows_ref)


def mlp_bwd(full, x, gy, small, wi, wo, z, slope, tile=512):
    rows, width = x.shape
    hidden = 2 * wi.shape[2]
    steps = hidden // tile
    whole = pl.BlockSpec((rows, width), lambda g: (0, 0))
    part = pl.BlockSpec((rows, tile), lambda g: (0, g))
    wi_spec = pl.BlockSpec((None, width, tile), lambda g: (g // (steps // 2), 0, g % (steps // 2)))
    dwi_spec = pl.BlockSpec((width, tile), lambda g: (0, g))
    wo_spec = pl.BlockSpec((tile, width), lambda g: (g, 0))
    out_shape = [jax.ShapeDtypeStruct((rows, width), BF16)]
    out_specs = [whole]
    scratch = [pltpu.VMEM((rows, width), F32)]
    if full:
        out_shape += [
            jax.ShapeDtypeStruct((8, width), F32),
            jax.ShapeDtypeStruct((1, hidden), F32),
            jax.ShapeDtypeStruct((width, hidden), BF16),
            jax.ShapeDtypeStruct((hidden, width), BF16),
        ]
        out_specs += [
            pl.BlockSpec((8, width), lambda g: (0, 0)),
            pl.BlockSpec((1, tile), lambda g: (0, g)),
            dwi_spec,
            wo_spec,
        ]
        scratch += [pltpu.VMEM((width, rows), BF16)]
    return pl.pallas_call(
        functools.partial(mlp_bwd_kernel, full),
        grid=(steps,),
        in_specs=[whole, whole, pl.BlockSpec((7, width), lambda g: (0, 0)), wi_spec, wo_spec, part, part],
        out_specs=out_specs,
        out_shape=out_shape,
        scratch_shapes=scratch,
        compiler_params=pltpu.CompilerParams(vmem_limit_bytes=VMEM_LIMIT),
        cost_estimate=pl.CostEstimate(
            flops=(8 if full else 4) * rows * width * hidden,
            bytes_accessed=(8 if full else 4) * width * hidden + 6 * rows * width + 4 * rows * hidden,
            transcendentals=0,
        ),
        name="mlp_bwd_full" if full else "mlp_bwd_act",
    )(x, gy, small, wi, wo, z, slope)


def attn_bwd_kernel(
    full, x_ref, gy_ref, small_ref, wq_ref, wk_ref, wv_ref, wo_ref, cos_ref, sin_ref,
    q_ref, k_ref, v_ref, e_ref, linv_ref, o_ref, grid_ref, gx_ref, *rest
):
    if full:
        rows_ref, bias_ref, angle_ref, dwq_ref, dwk_ref, dwv_ref, dwo_ref, du_s, ut_s = rest
    else:
        rows_ref = None
        (du_s,) = rest
    step = pl.program_id(0)

    @pl.when(step == 0)
    def _():
        du_s[...] = jnp.zeros_like(du_s)
        if full:
            normed, _ = normalize(x_ref[...].astype(F32))
            lowered = (normed * small_ref[0:1] + small_ref[1:2]).astype(BF16)
            ut_s[...] = lowered.T

    gy = gy_ref[...]
    width = q_ref.shape[1]
    scale = HD ** (-0.5)
    low_lane = lane_index(2 * HD) < HD
    do_all = dot_t(gy, wo_ref[...])
    o_all = o_ref[...]
    if full:
        dwo_ref[...] = tdot(o_all.astype(BF16), gy).astype(BF16)
    dos_all = (do_all * linv_ref[...]).astype(BF16)
    parts = []
    for pair in range(width // (2 * HD)):
        lanes = slice(pair * 2 * HD, (pair + 1) * 2 * HD)
        qp, kp, vp = q_ref[:, lanes], k_ref[:, lanes], v_ref[:, lanes]
        dos = dos_all[:, lanes]
        product = dos.astype(F32) * o_all[:, lanes]
        zero = jnp.zeros_like(qp)
        dq = dk = dv = 0.0
        for half in range(2):
            mine = low_lane if half == 0 else jnp.logical_not(low_lane)
            offset = jnp.sum(jnp.where(mine, product, 0.0), axis=-1, keepdims=True)
            dos_h = jnp.where(mine, dos, zero)
            e = e_ref[pair * 2 + half]
            dp = dot_t(dos_h, vp)
            ds = (e.astype(F32) * (dp - offset)).astype(BF16)
            dv = dv + tdot(e, dos_h)
            dq = dq + dot(ds, jnp.where(mine, kp, zero))
            dk = dk + tdot(ds, jnp.where(mine, qp, zero))
        parts.append((dq * scale, dk * scale, dv))
    dqr = jnp.concatenate([p[0] for p in parts], axis=1)
    dkr = jnp.concatenate([p[1] for p in parts], axis=1)
    dv = jnp.concatenate([p[2] for p in parts], axis=1).astype(BF16)
    cosine, sine = cos_ref[...], sin_ref[...]
    dq = (dqr * cosine - swap_halves(dqr) * sine).astype(BF16)
    dk = (dkr * cosine - swap_halves(dkr) * sine).astype(BF16)
    du_s[...] += dot_t(dq, wq_ref[...]) + dot_t(dk, wk_ref[...]) + dot_t(dv, wv_ref[...])
    if full:
        turned = dqr * swap_halves(q_ref[...].astype(F32)) + dkr * swap_halves(k_ref[...].astype(F32))
        angle_ref[0:1] = jnp.sum(turned * grid_ref[:, 0:1], axis=0, keepdims=True)
        angle_ref[1:2] = jnp.sum(turned * grid_ref[:, 1:2], axis=0, keepdims=True)
        bias_ref[0:1] = jnp.sum(dq.astype(F32), axis=0, keepdims=True)
        bias_ref[1:2] = jnp.sum(dk.astype(F32), axis=0, keepdims=True)
        bias_ref[2:3] = jnp.sum(dv.astype(F32), axis=0, keepdims=True)
        ut = ut_s[...]
        dwq_ref[...] = dot(ut, dq).astype(BF16)
        dwk_ref[...] = dot(ut, dk).astype(BF16)
        dwv_ref[...] = dot(ut, dv).astype(BF16)

    @pl.when(step == pl.num_programs(0) - 1)
    def _():
        norm_back(full, x_ref, gy_ref, small_ref, du_s[...], gx_ref, rows_ref)


def attn_bwd(full, x, gy, small, w, cos, sin, saved, grid_pos):
    rows, width = x.shape
    group = 4 * HD
    steps = width // group
    heads = width // HD
    whole = pl.BlockSpec((rows, width), lambda g: (0, 0))
    part = pl.BlockSpec((rows, group), lambda g: (0, g))

    def wcol(base):
        return pl.BlockSpec(
            (None, width, group), lambda g, base=base: (base // 2, 0, base % 2 * steps + g)
        )

    strip = pl.BlockSpec((8, group), lambda g: (0, g))
    out_shape = [jax.ShapeDtypeStruct((rows, width), BF16)]
    out_specs = [whole]
    scratch = [pltpu.VMEM((rows, width), F32)]
    if full:
        out_shape += [jax.ShapeDtypeStruct((8, width), F32)] * 3
        out_shape += [jax.ShapeDtypeStruct((width, width), BF16)] * 4
        out_specs += [pl.BlockSpec((8, width), lambda g: (0, 0)), strip, strip]
        out_specs += [pl.BlockSpec((width, group), lambda g: (0, g))] * 3
        out_specs += [pl.BlockSpec((group, width), lambda g: (g, 0))]
        scratch += [pltpu.VMEM((width, rows), BF16)]
    q, k, v, e, linv, o = saved
    return pl.pallas_call(
        functools.partial(attn_bwd_kernel, full),
        grid=(steps,),
        in_specs=[
            whole, whole,
            pl.BlockSpec((7, width), lambda g: (0, 0)),
            wcol(0), wcol(1), wcol(2),
            pl.BlockSpec((None, group, width), lambda g: (1, g, 1)),
            part, part, part, part, part,
            pl.BlockSpec((4, rows, rows), lambda g: (g, 0, 0)),
            part, part,
            pl.BlockSpec((rows, 128), lambda g: (0, 0)),
        ],
        out_specs=out_specs,
        out_shape=out_shape,
        scratch_shapes=scratch,
        compiler_params=pltpu.CompilerParams(vmem_limit_bytes=VMEM_LIMIT),
        cost_estimate=pl.CostEstimate(
            flops=(4 if full else 2) * rows * width * 4 * width + 16 * 4 * rows * rows * width,
            bytes_accessed=(16 if full else 8) * width * width + 30 * rows * width + 2 * heads * rows * rows,
            transcendentals=0,
        ),
        name="attn_bwd_full" if full else "attn_bwd_act",
    )(x, gy, small, w, w, w, w, cos, sin, q, k, v, e, linv, o, grid_pos)


NEXT_LAYER = ((0, 2), (1, 3))
PREV_LAYER = ((2, 0), (3, 1))
SIBLING = ((0, 1), (1, 0), (2, 3), (3, 2))
FROM_MLP = ((1, 0), (3, 2))
FROM_ATTN = ((0, 1), (2, 3))
MOMENTUM = 0.9
DECAY = 0.0001
AVERAGE = 0.8
RATE = 0.03
MASKED = -1e30


def sibling(value):
    return lax.ppermute(value, "section", SIBLING)


class Ring:
    def __init__(self, size):
        self.size = size
        self.order = list(range(0, size, 2)) + list(range(size - 1 - size % 2, 0, -2))
        place = [0] * size
        for at, member in enumerate(self.order):
            place[member] = at
        self.order_table = jnp.array(self.order, jnp.int32)
        self.at = jnp.array(place, jnp.int32)[lax.axis_index("dp")]
        self.right = [(self.order[i], self.order[(i + 1) % size]) for i in range(size)]
        self.left = [(b, a) for a, b in self.right]

    def member(self, offset):
        return self.order_table[(self.at + offset + 2 * self.size) % self.size]

    def to_right(self, value):
        return lax.ppermute(value, "dp", self.right)

    def to_left(self, value):
        return lax.ppermute(value, "dp", self.left)


def gather_parts(ring, shard):
    parts = [(shard, 0, None)]
    reach = ring.size // 2
    rightward = leftward = shard
    for step in range(1, reach):
        rightward = ring.to_right(rightward)
        leftward = ring.to_left(leftward)
        parts += [(rightward, -step, None), (leftward, step, None)]
    middle = shard.shape[-1] // 2
    parts.append((ring.to_right(rightward[..., :middle]), -reach, 0))
    parts.append((ring.to_left(leftward[..., middle:]), reach, 1))
    return parts


def place_kernel(layout, count, place_ref, *refs):
    sources, target, semaphores = refs[:count], refs[count], refs[count + 1]
    copies = []
    for number, (source, (side, part)) in enumerate(zip(sources, layout)):
        spot = place_ref[number]
        half = place_ref[count + side]
        if target.shape[1] == 2:
            place = target.at[spot, half]
        else:
            place = target.at[half, spot]
        if part is not None:
            length = source.shape[-1]
            place = place.at[:, pl.ds(part * length, length)]
        copies.append(pltpu.make_async_copy(source, place, semaphores.at[number]))
    for copy in copies:
        copy.start()
    for copy in copies:
        copy.wait()


def gather_weight(ring, core, shard, spot_first):
    mine = gather_parts(ring, shard)
    arrays, layout, places = [], [], []
    for value, offset, part in mine:
        for side, held in ((0, value), (1, sibling(value))):
            arrays.append(held)
            layout.append((side, part))
            places.append(ring.member(offset))
    count = len(arrays)
    table = jnp.stack(places + [core, 1 - core]).astype(jnp.int32)
    rows, columns = shard.shape
    if spot_first:
        shape = (ring.size, 2, rows, columns)
    else:
        shape = (2, ring.size, rows, columns)
    fitted = pl.pallas_call(
        functools.partial(place_kernel, tuple(layout), count),
        in_specs=[pl.BlockSpec(memory_space=pltpu.SMEM)] + [pl.BlockSpec(memory_space=pl.ANY)] * count,
        out_specs=pl.BlockSpec(memory_space=pl.ANY),
        out_shape=jax.ShapeDtypeStruct(shape, shard.dtype),
        scratch_shapes=[pltpu.SemaphoreType.DMA((count,))],
        cost_estimate=pl.CostEstimate(
            flops=0, bytes_accessed=8 * ring.size * rows * columns, transcendentals=0
        ),
        name="place_weight",
    )(table, *arrays)
    if spot_first:
        return fitted.reshape(2 * ring.size * rows, columns)
    return fitted.reshape(2, ring.size * rows, columns)


def reduce_over_ring(ring, chunks):
    reach = ring.size // 2

    def own(offset):
        return lax.dynamic_index_in_dim(chunks, ring.member(offset), 0, keepdims=False)

    middle = chunks.shape[-1] // 2
    far = own(reach)
    rightward = ring.to_right(far[..., :middle])
    leftward = ring.to_left(far[..., middle:])
    for step in range(1, reach):
        term_r, term_l = own(reach - step), own(step - reach)
        if step == 1:
            rightward = jnp.concatenate([term_r[..., :middle] + rightward, term_r[..., middle:]], axis=-1)
            leftward = jnp.concatenate([term_l[..., :middle], term_l[..., middle:] + leftward], axis=-1)
        else:
            rightward, leftward = term_r + rightward, term_l + leftward
        rightward, leftward = ring.to_right(rightward), ring.to_left(leftward)
    return own(0).astype(F32) + rightward.astype(F32) + leftward.astype(F32)


def sum_over_dp(value):
    size = lax.axis_size("dp")
    bit = 1
    while bit < size:
        value = value + lax.ppermute(value, "dp", [(i, i ^ bit) for i in range(size)])
        bit *= 2
    return value


def advance(master, moment, average, gradient, step_rate):
    gradient = gradient + DECAY * master
    moment = MOMENTUM * moment + gradient
    master = master - step_rate * (gradient + MOMENTUM * moment)
    average = AVERAGE * average + (1 - AVERAGE) * master
    return (moment, master, average)


def on_device(
    block_input, out_cotangent, segment_ids, grid_row, grid_col, valid_slot,
    in_master, out_master, in_moment, out_moment, in_average, out_average,
    small_master, small_moment, small_average,
):
    section_index = lax.axis_index("section")
    layer, core = section_index // 2, section_index % 2
    first_core = core == 0
    first_layer = layer == 0
    micro_count, row_count, width = block_input.shape
    ring = Ring(lax.axis_size("dp"))

    def mine(source):
        return lax.dynamic_index_in_dim(source, core, 0, keepdims=False)

    def by_core(if_first, if_second):
        return jnp.where(first_core, if_first, if_second)

    in_low = in_master[0].astype(BF16)
    out_low = out_master[0].astype(BF16)
    in_rows, hidden = in_low.shape
    out_rows = out_low.shape[0]
    in_half, out_half = hidden // 2, out_rows // 2
    crossed = sibling(by_core(in_low[:, in_half:], in_low[:, :in_half]))
    attn_shard = by_core(in_low[:, :in_half], crossed)
    up_shard = by_core(crossed, in_low[:, in_half:])
    down_shard = by_core(lax.ppermute(out_low[:out_half], "section", FROM_MLP), out_low[out_half:])
    small_own = small_master[0]
    small_other = sibling(small_own)
    small_attn = by_core(small_own, small_other)
    small_mlp = by_core(small_other, small_own)
    w_attn = gather_weight(ring, core, attn_shard, False)
    w_up = gather_weight(ring, core, up_shard, False)
    w_down = gather_weight(ring, core, down_shard, True)

    seg, row_at, col_at, valid = (mine(m) for m in (segment_ids, grid_row, grid_col, valid_slot))
    head_count = width // HD
    frequency = small_attn[6].reshape(head_count, 2, 1, HD // 2)
    spread = jnp.broadcast_to(frequency, (head_count, 2, 2, HD // 2))
    angle = (
        col_at.astype(F32)[:, None] * spread[:, 0].reshape(1, width)
        + row_at.astype(F32)[:, None] * spread[:, 1].reshape(1, width)
    )
    turn_sign = jnp.where(lax.broadcasted_iota(jnp.int32, (1, width), 1) % HD < HD // 2, -1.0, 1.0)
    cosine = jnp.cos(angle)
    sine = jnp.sin(angle) * turn_sign
    tag = lax.broadcasted_iota(jnp.int32, (1, 128), 1)
    same = seg[:, None] == tag
    query_tag = same.astype(BF16)
    key_tag = jnp.where(same & (valid[:, None] > 0), 0.0, MASKED).astype(BF16)
    lane = lax.broadcasted_iota(jnp.int32, (1, 128), 1)
    grid_pos = jnp.where(lane == 0, col_at.astype(F32)[:, None], row_at.astype(F32)[:, None])
    x0 = mine(block_input)
    cotangent = mine(out_cotangent) * valid.astype(BF16)[:, None]

    (mid0,) = attn_fwd(False, x0, small_attn, w_attn, cosine, sine, query_tag, key_tag)
    (top0,) = mlp_fwd(False, mid0, small_mlp, w_up, w_down)
    entering = jnp.where(first_layer, x0, lax.ppermute(top0, "section", NEXT_LAYER))

    mid, *saved = attn_fwd(True, entering, small_attn, w_attn, cosine, sine, query_tag, key_tag)
    top, z, slope = mlp_fwd(True, mid, small_mlp, w_up, w_down)

    (back_mid,) = mlp_bwd(False, mid, cotangent, small_mlp, w_up, w_down, z, slope)
    (back_in,) = attn_bwd(False, entering, back_mid, small_attn, w_attn, cosine, sine, saved, grid_pos)
    arriving = jnp.where(first_layer, lax.ppermute(back_in, "section", PREV_LAYER), cotangent)

    grad_mid, mlp_rows, up_bias, d_up, d_down = mlp_bwd(
        True, mid, arriving, small_mlp, w_up, w_down, z, slope
    )
    kept_up = by_core(d_up[:, :in_half], d_up[:, in_half:])
    sent_up = by_core(d_up[:, in_half:], d_up[:, :in_half])
    up_sum = kept_up + sibling(sent_up)
    up_share = reduce_over_ring(ring, up_sum.reshape(ring.size, in_rows, in_half))
    d_down = d_down.reshape(ring.size, 2, out_half, width)
    kept_down = by_core(d_down[:, 0], d_down[:, 1])
    sent_down = by_core(d_down[:, 1], d_down[:, 0])
    down_sum = kept_down + sibling(sent_down)
    down_share = reduce_over_ring(ring, down_sum)

    grad_in, attn_rows, attn_bias, turned, d_q, d_k, d_v, d_o = attn_bwd(
        True, entering, grad_mid, small_attn, w_attn, cosine, sine, saved, grid_pos
    )
    first_sum = by_core(d_q, d_v) + sibling(by_core(d_v, d_q))
    second_sum = by_core(d_k, d_o) + sibling(by_core(d_o, d_k))
    first_share = reduce_over_ring(ring, first_sum.reshape(ring.size, in_rows, width))
    second_share = reduce_over_ring(ring, second_sum.reshape(ring.size, in_rows, width))
    attn_share = jnp.concatenate([first_share, second_share], axis=1)

    turned = turned[:2].reshape(2, head_count, 2, HD // 2)
    grad_frequency = jnp.transpose(turned[:, :, 1] - turned[:, :, 0], (1, 0, 2)).reshape(1, width)
    attn_small = jnp.concatenate([attn_rows[:2], attn_bias[:3], attn_rows[2:3], grad_frequency], axis=0)
    mlp_small = jnp.concatenate([mlp_rows[:2], up_bias.reshape(4, width), mlp_rows[2:3]], axis=0)
    small_grad = sum_over_dp(by_core(attn_small, mlp_small) + sibling(by_core(mlp_small, attn_small)))

    crossed = sibling(by_core(up_share, attn_share).astype(BF16)).astype(F32)
    share_in = jnp.concatenate([by_core(attn_share, crossed), by_core(crossed, up_share)], axis=1)
    crossed = lax.ppermute(down_share.astype(BF16), "section", FROM_ATTN).astype(F32)
    share_out = jnp.where(first_core, 0.0, jnp.concatenate([crossed, down_share], axis=0))

    step_rate = RATE / math.sqrt(lax.axis_size("dp") * micro_count * row_count)
    in_new = advance(in_master[0], in_moment[0], in_average[0], share_in, step_rate)
    out_new = advance(out_master[0], out_moment[0], out_average[0], share_out, step_rate)
    small_new = advance(small_own, small_moment[0], small_average[0], small_grad, step_rate)
    branch_bias = by_core(small_grad[5], small_grad[6])

    def both_micro(attn_value, mlp_value):
        kept = by_core(attn_value, mlp_value)
        crossed = sibling(by_core(mlp_value, attn_value))
        return jnp.stack([by_core(kept, crossed), by_core(crossed, kept)])

    outputs = both_micro(mid, top)
    input_grads = both_micro(grad_in, grad_mid)
    return tuple(
        value[None]
        for value in (outputs, input_grads, *in_new, *out_new, *small_new, branch_bias)
    )


def solution(mesh):
    rows = P(None, "dp", None)
    slots = P(None, "dp")
    matrix = P("section", "dp", None)
    vectors = P("section", None, None)
    return jax.shard_map(
        on_device,
        mesh=mesh,
        in_specs=(rows,) * 2 + (slots,) * 4 + (matrix,) * 6 + (vectors,) * 3,
        out_specs=(P("section", None, "dp", None),) * 2 + (matrix,) * 6 + (vectors,) * 3 + (P("section", None),),
        check_vma=False,
    )
```

time: 1590 us -> 910 us (0.57)
  waiting for transfers between devices: 773 us -> 137 us
  Pallas kernels: 0 us -> 593 us
  matrix products: 260 us -> 0 us
  local copies, waits for them, and re-layouts: 186 us -> 34.5 us
  other arithmetic: 185 us -> 34.6 us
  loops' own time: 70.4 us -> 0 us
  blocking collectives: 37.1 us -> 0 us
  starting transfers between devices: 53.8 us -> 81 us
    pallas_call x0 -> x11, Pallas kernels: none -> 593 us  [the longest x3 435 us: gather_weight(): pl.pallas_call(functools.partial(place_kernel, tuple(layout), count), in_...]
    ppermute x8 -> x100, waiting for transfers between devices: 375 us -> 137 us  [the longest x28 71.3 us: to_right(): return lax.ppermute(value, 'dp', self.right)]
    psum x1 -> x0, waiting for transfers between devices: 237 us -> none  [on_device(): lax.psum(grad_in_total.astype(jnp.bfloat16), 'dp').astype(jnp.float32)]
    dot_general x54 -> x0, matrix products: 163 us -> none  [the longest x12 42.4 us: one_group(): jnp.einsum('hqk,khd->qhd', attend_weights, take_group(values, offset), pr...]
    all_gather x2 -> x0, waiting for transfers between devices: 161 us -> none  [the longest x1 80.8 us: on_device(): lax.all_gather(out_master.astype(jnp.bfloat16), 'dp', axis=1, tiled=True)]
    sub x18 -> x0, matrix products: 97.4 us -> none  [head_probs(): exponent = jnp.exp(masked_scores - top_score)]
    another operation x16 -> x0, loops' own time: 70.4 us -> none  [the longest x5 35.4 us: on_device(): lax.switch(chosen, (spare_backward, attention_backward, mlp_backward), en...]
    dynamic_slice x68 -> x3, local copies, waits for them, and re-layouts: 52.1 us -> 1.31 us  [the longest x1 0.71 us: member(): return self.order_table[(self.at + offset + 2 * self.size) % self.size]]
  transfers between devices with their start and end apart: 11 -> 100, of which waited for: 10 -> 41; matrix products, arithmetic and copies ran while one was open for 2% -> 6% of each run, Pallas kernels for 0% -> 40%
where the time goes in v1:
time: 910 us; the launch traced here: 903 us
  Pallas kernels  593 us (65%)
  waiting for transfers between devices  137 us (15%)
  starting transfers between devices  81 us (9%)
  other arithmetic  34.6 us (4%)
  local copies, waits for them, and re-layouts  34.5 us (4%)
  between operations  23.4 us (3%)
    pallas_call x3, Pallas kernels, gather_weight(): pl.pallas_call(functools.partial(place_kernel, tuple(layout), count), in_...  435 us
    ppermute x28, waiting for transfers between devices, to_right(): return lax.ppermute(value, 'dp', self.right)  71.3 us
    pallas_call x2, Pallas kernels, attn_bwd(): pl.pallas_call(functools.partial(attn_bwd_kernel, full), grid=(steps,), i...  55.1 us
    pallas_call x2, Pallas kernels, attn_fwd(): pl.pallas_call(functools.partial(attn_fwd_kernel, save), grid=(steps,), i...  40.7 us
    pallas_call x2, Pallas kernels, mlp_bwd(): pl.pallas_call(functools.partial(mlp_bwd_kernel, full), grid=(steps,), in...  35.9 us
    ppermute x28, starting transfers between devices, to_left(): return lax.ppermute(value, 'dp', self.left)  33.7 us
    ppermute x28, waiting for transfers between devices, to_left(): return lax.ppermute(value, 'dp', self.left)  32.2 us
    pallas_call x2, Pallas kernels, mlp_fwd(): pl.pallas_call(functools.partial(mlp_fwd_kernel, save), grid=(steps,), in...  26.4 us
  transfers between devices with their start and end apart: 100, of which 41 were waited for; matrix products, arithmetic and copies ran while one was open for 6% of the time, Pallas kernels for 40%

profile of v1, /device:TPU:0, one launch (start us, length us, event | category | flops | bytes accessed | tf_op | source)
XLA Modules:
  0.0 903.4 jit_solution(9674630949257126855)
XLA Ops:
  11.0 5.5 collective-permute-done.38.refs_2_
  58.4 11.9 %stack.35.place_ref = s32[20]{0:T(128)} concatenate(s32[1]{0:T(128)} %get-tuple-element.149, s32[1]{0:T(128)} %get-tuple-element.149, s32[1]{0:T(128)} %get-tuple-element.148, s32[1]{0:T(128)} %get-tuple-element.148, s32[1]{0:T(128)} %get-tuple-element.147, s32[1]{0:T(128)} %get-tuple-element.147, s32[1]{0:T(128)} %get-tuple-element.146, s32[1]{0:T(128)} %get-tuple-element.146, ...), dimensions={0} | concatenate | bytes 160 | tf_op jit(solution)/shard_map/stack | solution.py:515
  75.1 7.0 collective-permute-done.28.refs_10_
  82.1 5.5 collective-permute-done.11.refs_10_
  104.3 8.5 sine_multiply_fusion
  117.4 144.9 %place_weight.3 = bf16[2,8,96,1536]{3,2,1,0:T(8,128)(2,1)} custom-call(s32[20]{0:T(128)} %stack.35.place_ref, bf16[96,1536]{1,0:T(8,128)(2,1)} %copy-done.20, bf16[96,1536]{1,0:T(8,128)(2,1)} %copy-done.40, bf16[96,1536]{1,0:T(8,128)(2,1)} %collective-permute-done.3.refs_2_, bf16[96,1536]{1,0:T(8,128)(2,1)} %collective-permute-done.4.refs_3_, ...), custom_call_target="tpu_custom_call" | custom-call | bytes 9437184 | tf_op jit(solution)/shard_map/place_weight/pallas_call | solution.py:521
  263.6 19.3 %attn_fwd.2.x_ref = bf16[640,768]{1,0:T(8,128)(2,1)} custom-call(bf16[640,768]{1,0:T(8,128)(2,1)} %dynamic-slice_bitcast_fusion.x_ref, f32[7,768]{1,0:T(8,128)} %copy-done.56, bf16[2,768,1536]{2,1,0:T(8,128)(2,1)} %bitcast.220, bf16[2,768,1536]{2,1,0:T(8,128)(2,1)} %bitcast.221, bf16[2,768,1536]{2,1,0:T(8,128)(2,1)} %bitcast.222, ...), custom_call_target="tpu_custom_call" | custom-call | flops 8053063680 | bytes 6684672 | tf_op jit(solution)/shard_map/attn_fwd/pallas_call | solution.py:138
  282.9 144.9 %place_weight.5 = bf16[8,2,192,768]{3,2,1,0:T(8,128)(2,1)} custom-call(s32[20]{0:T(128)} %stack.35.place_ref, bf16[192,768]{1,0:T(8,128)(2,1)} %copy-done.18, bf16[192,768]{1,0:T(8,128)(2,1)} %copy-done.33, bf16[192,768]{1,0:T(8,128)(2,1)} %copy-done.30, bf16[192,768]{1,0:T(8,128)(2,1)} %copy-done.38, bf16[192,768]{1,0:T(8,128)(2,1)} %copy-done.32, ...), custom_call_target="tpu_custom_call" | custom-call | bytes 9437184 | tf_op jit(solution)/shard_map/place_weight/pallas_call | solution.py:521
  429.4 144.9 %place_weight.4 = bf16[2,8,96,1536]{3,2,1,0:T(8,128)(2,1)} custom-call(s32[20]{0:T(128)} %stack.35.place_ref, bf16[96,1536]{1,0:T(8,128)(2,1)} %copy-done.19, bf16[96,1536]{1,0:T(8,128)(2,1)} %copy-done.31, bf16[96,1536]{1,0:T(8,128)(2,1)} %collective-permute-done.20.refs_2_, bf16[96,1536]{1,0:T(8,128)(2,1)} %collective-permute-done.21.refs_3_, ...), custom_call_target="tpu_custom_call" | custom-call | bytes 9437184 | tf_op jit(solution)/shard_map/place_weight/pallas_call | solution.py:521
  574.3 12.1 %mlp_fwd.2 = bf16[640,768]{1,0:T(8,128)(2,1)} custom-call(bf16[640,768]{1,0:T(8,128)(2,1)} %attn_fwd.2.x_ref, f32[7,768]{1,0:T(8,128)} %copy-done.57, f32[1,3072]{1,0:T(1,128)} %bitcast.245, bf16[2,768,1536]{2,1,0:T(8,128)(2,1)} %bitcast.240, bf16[3072,768]{1,0:T(8,128)(2,1)} %bitcast.236), custom_call_target="tpu_custom_call" | custom-call | flops 6039797760 | bytes 11403264 | tf_op jit(solution)/shard_map/mlp_fwd/pallas_call | solution.py:200
  586.4 4.8 collective-permute-start.54
  593.3 18.4 %collective-permute-done.54 = bf16[640,768]{1,0:T(8,128)(2,1)} collective-permute-done((bf16[640,768]{1,0:T(8,128)(2,1)}, bf16[640,768]{1,0:T(8,128)(2,1)}, u32[]{:S(2)}, u32[]{:S(2)}) %collective-permute-start.54) | collective-permute-done | bytes 983072 | tf_op jit(solution)/shard_map/ppermute | solution.py:632
  612.9 21.4 %attn_fwd.3 = (bf16[640,768]{1,0:T(8,128)(2,1)}, bf16[640,768]{1,0:T(8,128)(2,1)}, bf16[640,768]{1,0:T(8,128)(2,1)}, bf16[640,768]{1,0:T(8,128)(2,1)}, bf16[12,6...) custom-call(bf16[640,768]{1,0:T(8,128)(2,1)} %broadcast_select_fusion.4.x_ref, f32[7,768]{1,0:T(8,128)} %copy-done.56, ...), custom_call_target="tpu_custom_call" | custom-call | flops 8053063680 | bytes 6684672 | tf_op jit(solution)/shard_map/attn_fwd/pallas_call | solution.py:138
  634.3 14.3 %mlp_fwd.3 = (bf16[640,768]{1,0:T(8,128)(2,1)}, bf16[640,3072]{1,0:T(8,128)(2,1)}, bf16[640,3072]{1,0:T(8,128)(2,1)}) custom-call(bf16[640,768]{1,0:T(8,128)(2,1)} %get-tuple-element.35.x_ref, f32[7,768]{1,0:T(8,128)} %copy-done.57, f32[1,3072]{1,0:T(1,128)} %bitcast.246, bf16[2,768,1536]{2,1,0:T(8,128)(2,1)} %bitcast.241, bf16[3072,768]{1,0:T(8,128)(2,1)} %bitcast.237), custom_call_target="tpu_custom_call" | custom-call | flops 6039797760 | bytes 11403264 | tf_op jit(solution)/shard_map/mlp_fwd/pallas_call | solution.py:200
  648.6 14.2 %mlp_bwd_act.1.gy_ref = bf16[640,768]{1,0:T(8,128)(2,1)} custom-call(bf16[640,768]{1,0:T(8,128)(2,1)} %get-tuple-element.35.x_ref, bf16[640,768]{1,0:T(8,128)(2,1)} %bitcast_multiply_fusion.gy_ref, f32[7,768]{1,0:T(8,128)} %copy-done.57, bf16[2,768,1536]{2,1,0:T(8,128)(2,1)} %bitcast.242, bf16[3072,768]{1,0:T(8,128)(2,1)} %bitcast.238, ...), custom_call_target="tpu_custom_call" | custom-call | flops 6039797760 | bytes 20250624 | tf_op jit(solution)/shard_map/mlp_bwd_act/pallas_call | solution.py:295
  662.7 25.1 %attn_bwd_act.1 = bf16[640,768]{1,0:T(8,128)(2,1)} custom-call(bf16[640,768]{1,0:T(8,128)(2,1)} %broadcast_select_fusion.4.x_ref, bf16[640,768]{1,0:T(8,128)(2,1)} %mlp_bwd_act.1.gy_ref, f32[7,768]{1,0:T(8,128)} %copy-done.56, bf16[2,768,1536]{2,1,0:T(8,128)(2,1)} %bitcast.228, bf16[2,768,1536]{2,1,0:T(8,128)(2,1)} %bitcast.229, ...), custom_call_target="tpu_custom_call" | custom-call | flops 23152558080 | bytes 29294592 | tf_op jit(solution)/shard_map/attn_bwd_act/pallas_call | solution.py:408
  705.1 9.5 %collective-permute-done.56 = bf16[640,768]{1,0:T(8,128)(2,1)} collective-permute-done((bf16[640,768]{1,0:T(8,128)(2,1)}, bf16[640,768]{1,0:T(8,128)(2,1)}, u32[]{:S(2)}, u32[]{:S(2)}) %collective-permute-start.56) | collective-permute-done | bytes 983072 | tf_op jit(solution)/shard_map/ppermute | solution.py:639
  717.0 21.8 %mlp_bwd_full.1 = (bf16[640,768]{1,0:T(8,128)(2,1)}, f32[8,768]{1,0:T(8,128)}, f32[1,3072]{1,0:T(1,128)}, bf16[768,3072]{1,0:T(8,128)(2,1)}, bf16[3072,768]{1,0:T(8,128)(2,1)}) custom-call(bf16[640,768]{1,0:T(8,128)(2,1)} %get-tuple-element.35.x_ref, bf16[640,768]{1,0:T(8,128)(2,1)} %broadcast_select_fusion.3.gy_ref, f32[7,768]{1,0:T(8,128)} %copy-done.57, ...), custom_call_target="tpu_custom_call" | custom-call | flops 12079595520 | bytes 29687808 | tf_op jit(solution)/shard_map/mlp_bwd_full/pallas_call | solution.py:295
  738.8 30.0 %attn_bwd_full.1 = (bf16[640,768]{1,0:T(8,128)(2,1)}, f32[8,768]{1,0:T(8,128)}, f32[8,768]{1,0:T(8,128)}, f32[8,768]{1,0:T(8,128)}, bf16[768,768]{1,0:T(8,128)(2...) custom-call(bf16[640,768]{1,0:T(8,128)(2,1)} %broadcast_select_fusion.4.x_ref, ...), custom_call_target="tpu_custom_call" | custom-call | flops 26172456960 | bytes 34013184 | tf_op jit(solution)/shard_map/attn_bwd_full/pallas_call | solution.py:408
  812.7 4.8 collective-permute-done.69
  845.0 8.6 collective-permute-done.88
  853.6 6.3 collective-permute-done.78
  862.5 6.3 collective-permute-done.89
  878.3 5.2 collective-permute-done.93
  (445 shorter events, 185.0 us)
Async XLA Ops:
  41.4 30.1 %collective-permute-start.4 = (bf16[96,1536]{1,0:T(8,128)(2,1)}, bf16[96,1536]{1,0:T(8,128)(2,1)}, u32[]{:S(2)}, u32[]{:S(2)}) collective-permute-start(bf16[96,1536]{1,0:T(8,128)(2,1)} %collective-permute-done.3.refs_2_), channel_id=1, source_target_pairs={{0,8},{8,0},{16,24},{24,16},{1,9},{9,1},{17,25},{25,17},{2,10},{10... | collective-permute-start | bytes 884744 | tf_op jit(solution)/shard_map/ppermute | solution.py:447
  43.8 27.6 %collective-permute-start.9 = (bf16[96,1536]{1,0:T(8,128)(2,1)}, bf16[96,1536]{1,0:T(8,128)(2,1)}, u32[]{:S(2)}, u32[]{:S(2)}) collective-permute-start(bf16[96,1536]{1,0:T(8,128)(2,1)} %collective-permute-done.5.refs_4_), channel_id=1, source_target_pairs={{2,0},{4,2},{6,4},{7,6},{5,7},{3,5},{1,3},{0,1},{10,8},{12,10},{14... | collective-permute-start | bytes 884744 | tf_op jit(solution)/shard_map/ppermute | solution.py:469
  45.2 26.7 %collective-permute-start.6 = (bf16[96,1536]{1,0:T(8,128)(2,1)}, bf16[96,1536]{1,0:T(8,128)(2,1)}, u32[]{:S(2)}, u32[]{:S(2)}) collective-permute-start(bf16[96,1536]{1,0:T(8,128)(2,1)} %collective-permute-done.5.refs_4_), channel_id=1, source_target_pairs={{0,8},{8,0},{16,24},{24,16},{1,9},{9,1},{17,25},{25,17},{2,10},{10... | collective-permute-start | bytes 884744 | tf_op jit(solution)/shard_map/ppermute | solution.py:447
  45.3 27.2 %collective-permute-start.46 = (bf16[192,768]{1,0:T(8,128)(2,1)}, bf16[192,768]{1,0:T(8,128)(2,1)}, u32[]{:S(2)}, u32[]{:S(2)}) collective-permute-start(bf16[192,768]{1,0:T(8,128)(2,1)} %copy-done.34), channel_id=1, source_target_pairs={{0,2},{2,4},{4,6},{6,7},{7,5},{5,3},{3,1},{1,0},{8,10},{10,12},{12... | collective-permute-start | bytes 884744 | tf_op jit(solution)/shard_map/ppermute | solution.py:466
  48.7 24.8 %collective-permute-start.48 = (bf16[192,768]{1,0:T(8,128)(2,1)}, bf16[192,768]{1,0:T(8,128)(2,1)}, u32[]{:S(2)}, u32[]{:S(2)}) collective-permute-start(bf16[192,768]{1,0:T(8,128)(2,1)} %copy-done.36), channel_id=1, source_target_pairs={{2,0},{4,2},{6,4},{7,6},{5,7},{3,5},{1,3},{0,1},{10,8},{12,10},{14... | collective-permute-start | bytes 884744 | tf_op jit(solution)/shard_map/ppermute | solution.py:469
  102.0 161.0 %collective-permute-start.47 = (bf16[192,768]{1,0:T(8,128)(2,1)}, bf16[192,768]{1,0:T(8,128)(2,1)}, u32[]{:S(2)}, u32[]{:S(2)}) collective-permute-start(bf16[192,768]{1,0:T(8,128)(2,1)} %collective-permute-done.46.refs_10_), channel_id=1, source_target_pairs={{0,8},{8,0},{16,24},{24,16},{1,9},{9,1},{17,25},{25,17},{2,10},{10... | collective-permute-start | bytes 884744 | tf_op jit(solution)/shard_map/ppermute | solution.py:447
  102.2 161.3 %collective-permute-start.49 = (bf16[192,768]{1,0:T(8,128)(2,1)}, bf16[192,768]{1,0:T(8,128)(2,1)}, u32[]{:S(2)}, u32[]{:S(2)}) collective-permute-start(bf16[192,768]{1,0:T(8,128)(2,1)} %collective-permute-done.48.refs_12_), channel_id=1, source_target_pairs={{0,8},{8,0},{16,24},{24,16},{1,9},{9,1},{17,25},{25,17},{2,10},{10... | collective-permute-start | bytes 884744 | tf_op jit(solution)/shard_map/ppermute | solution.py:447
  112.8 149.4 %collective-permute-start.34 = (bf16[96,768]{1,0:T(8,128)(2,1)S(1)}, bf16[96,768]{1,0:T(8,128)(2,1)S(1)}, u32[]{:S(2)}, u32[]{:S(2)}) collective-permute-start(bf16[96,768]{1,0:T(8,128)(2,1)S(1)} %slice.246), channel_id=1, source_target_pairs={{2,0},{4,2},{6,4},{7,6},{5,7},{3,5},{1,3},{0,1},{10,8},{12,10},{14... | collective-permute-start | bytes 442376 | tf_op jit(solution)/shard_map/ppermute | solution.py:469
  114.7 147.7 %collective-permute-start.51 = (bf16[192,384]{1,0:T(8,128)(2,1)}, bf16[192,384]{1,0:T(8,128)(2,1)S(1)}, u32[]{:S(2)}, u32[]{:S(2)}) collective-permute-start(bf16[192,384]{1,0:T(8,128)(2,1)} %collective-permute-done.50.refs_14_), channel_id=1, source_target_pairs={{0,8},{8,0},{16,24},{24,16},{1,9},{9,1},{17,25},{25,17},{2,10},{10... | collective-permute-start | bytes 442376 | tf_op jit(solution)/shard_map/ppermute | solution.py:447
  115.4 147.5 %collective-permute-start.53 = (bf16[192,384]{1,0:T(8,128)(2,1)}, bf16[192,384]{1,0:T(8,128)(2,1)S(1)}, u32[]{:S(2)}, u32[]{:S(2)}) collective-permute-start(bf16[192,384]{1,0:T(8,128)(2,1)} %collective-permute-done.52.refs_16_), channel_id=1, source_target_pairs={{0,8},{8,0},{16,24},{24,16},{1,9},{9,1},{17,25},{25,17},{2,10},{10... | collective-permute-start | bytes 442376 | tf_op jit(solution)/shard_map/ppermute | solution.py:447
  262.3 165.5 %collective-permute-start.27 = (bf16[96,1536]{1,0:T(8,128)(2,1)}, bf16[96,1536]{1,0:T(8,128)(2,1)S(1)}, u32[]{:S(2)}, u32[]{:S(2)}) collective-permute-start(bf16[96,1536]{1,0:T(8,128)(2,1)} %collective-permute-done.26.refs_8_), channel_id=1, source_target_pairs={{0,8},{8,0},{16,24},{24,16},{1,9},{9,1},{17,25},{25,17},{2,10},{10... | collective-permute-start | bytes 884744 | tf_op jit(solution)/shard_map/ppermute | solution.py:447
  262.4 165.5 %collective-permute-start.29 = (bf16[96,1536]{1,0:T(8,128)(2,1)S(1)}, bf16[96,1536]{1,0:T(8,128)(2,1)S(1)}, u32[]{:S(2)}, u32[]{:S(2)}) collective-permute-start(bf16[96,1536]{1,0:T(8,128)(2,1)S(1)} %collective-permute-done.28.refs_10_), channel_id=1, source_target_pairs={{0,8},{8,0},{16,24},{24,16},{1,9},{9,1},{17,25},{25,17},{2,10},{10... | collective-permute-start | bytes 884744 | tf_op jit(solution)/shard_map/ppermute | solution.py:447
  262.9 165.0 %collective-permute-start.31 = (bf16[96,1536]{1,0:T(8,128)(2,1)S(1)}, bf16[96,1536]{1,0:T(8,128)(2,1)S(1)}, u32[]{:S(2)}, u32[]{:S(2)}) collective-permute-start(bf16[96,1536]{1,0:T(8,128)(2,1)S(1)} %collective-permute-done.30.refs_12_), channel_id=1, source_target_pairs={{0,8},{8,0},{16,24},{24,16},{1,9},{9,1},{17,25},{25,17},{2,10},{10... | collective-permute-start | bytes 884744 | tf_op jit(solution)/shard_map/ppermute | solution.py:447
  263.0 164.8 %collective-permute-start.33 = (bf16[96,768]{1,0:T(8,128)(2,1)}, bf16[96,768]{1,0:T(8,128)(2,1)S(1)}, u32[]{:S(2)}, u32[]{:S(2)}) collective-permute-start(bf16[96,768]{1,0:T(8,128)(2,1)} %collective-permute-done.32.refs_14_), channel_id=1, source_target_pairs={{0,8},{8,0},{16,24},{24,16},{1,9},{9,1},{17,25},{25,17},{2,10},{10... | collective-permute-start | bytes 442376 | tf_op jit(solution)/shard_map/ppermute | solution.py:447
  263.5 164.3 %collective-permute-start.35 = (bf16[96,768]{1,0:T(8,128)(2,1)S(1)}, bf16[96,768]{1,0:T(8,128)(2,1)S(1)}, u32[]{:S(2)}, u32[]{:S(2)}) collective-permute-start(bf16[96,768]{1,0:T(8,128)(2,1)S(1)} %collective-permute-done.34.refs_16_), channel_id=1, source_target_pairs={{0,8},{8,0},{16,24},{24,16},{1,9},{9,1},{17,25},{25,17},{2,10},{10... | collective-permute-start | bytes 442376 | tf_op jit(solution)/shard_map/ppermute | solution.py:447
  586.4 25.3 %collective-permute-start.54 = (bf16[640,768]{1,0:T(8,128)(2,1)}, bf16[640,768]{1,0:T(8,128)(2,1)}, u32[]{:S(2)}, u32[]{:S(2)}) collective-permute-start(bf16[640,768]{1,0:T(8,128)(2,1)} %mlp_fwd.2), channel_id=1, source_target_pairs={{0,16},{8,24},{1,17},{9,25},{2,18},{10,26},{3,19},{11,27},{4,20},{... | collective-permute-start | bytes 2949128 | tf_op jit(solution)/shard_map/ppermute | solution.py:632
  687.8 26.8 %collective-permute-start.56 = (bf16[640,768]{1,0:T(8,128)(2,1)}, bf16[640,768]{1,0:T(8,128)(2,1)}, u32[]{:S(2)}, u32[]{:S(2)}) collective-permute-start(bf16[640,768]{1,0:T(8,128)(2,1)} %attn_bwd_act.1), channel_id=1, source_target_pairs={{16,0},{24,8},{17,1},{25,9},{18,2},{26,10},{19,3},{27,11},{20,4},{... | collective-permute-start | bytes 2949128 | tf_op jit(solution)/shard_map/ppermute | solution.py:639
  705.1 77.3 %collective-permute-start.55 = (bf16[640,768]{1,0:T(8,128)(2,1)}, bf16[640,768]{1,0:T(8,128)(2,1)}, u32[]{:S(2)}, u32[]{:S(2)}) collective-permute-start(bf16[640,768]{1,0:T(8,128)(2,1)} %broadcast_select_fusion.7), channel_id=1, source_target_pairs={{0,8},{8,0},{16,24},{24,16},{1,9},{9,1},{17,25},{25,17},{2,10},{10... | collective-permute-start | bytes 2949128 | tf_op jit(solution)/shard_map/ppermute | solution.py:447
  777.6 52.4 %collective-permute-start.86 = (bf16[8,192,768]{2,1,0:T(8,128)(2,1)S(1)}, bf16[8,192,768]{2,1,0:T(8,128)(2,1)S(1)}, u32[]{:S(2)}, u32[]{:S(2)}) collective-permute-start(bf16[8,192,768]{2,1,0:T(8,128)(2,1)S(1)} %select_bitcast_fusion), channel_id=1, source_target_pairs={{0,8},{8,0},{16,24},{24,16},{1,9},{9,1},{17,25},{25,17},{2,10},{10... | collective-permute-start | bytes 7077896 | tf_op jit(solution)/shard_map/ppermute | solution.py:447
  778.8 53.7 %collective-permute-start.76 = (bf16[768,1536]{1,0:T(8,128)(2,1)S(1)}, bf16[768,1536]{1,0:T(8,128)(2,1)S(1)}, u32[]{:S(2)}, u32[]{:S(2)}) collective-permute-start(bf16[768,1536]{1,0:T(8,128)(2,1)S(1)} %broadcast_select_fusion), channel_id=1, source_target_pairs={{0,8},{8,0},{16,24},{24,16},{1,9},{9,1},{17,25},{25,17},{2,10},{10... | collective-permute-start | bytes 7077896 | tf_op jit(solution)/shard_map/ppermute | solution.py:447
  823.6 51.9 %collective-permute-start.62 = (bf16[96,768]{1,0:T(8,128)(2,1)S(1)}, bf16[96,768]{1,0:T(8,128)(2,1)S(1)}, u32[]{:S(2)}, u32[]{:S(2)}) collective-permute-start(bf16[96,768]{1,0:T(8,128)(2,1)S(1)} %get-tuple-element.94), channel_id=1, source_target_pairs={{0,2},{2,4},{4,6},{6,7},{7,5},{5,3},{3,1},{1,0},{8,10},{10,12},{12... | collective-permute-start | bytes 442376 | tf_op jit(solution)/shard_map/ppermute | solution.py:466
  825.9 34.0 %collective-permute-start.74 = (bf16[96,768]{1,0:T(8,128)(2,1)S(1)}, bf16[96,768]{1,0:T(8,128)(2,1)S(1)}, u32[]{:S(2)}, u32[]{:S(2)}) collective-permute-start(bf16[96,768]{1,0:T(8,128)(2,1)S(1)} %get-tuple-element.100), channel_id=1, source_target_pairs={{2,0},{4,2},{6,4},{7,6},{5,7},{3,5},{1,3},{0,1},{10,8},{12,10},{14... | collective-permute-start | bytes 442376 | tf_op jit(solution)/shard_map/ppermute | solution.py:469
  837.3 23.6 %collective-permute-start.92 = (bf16[192,768]{1,0:T(8,128)(2,1)S(1)}, bf16[192,768]{1,0:T(8,128)(2,1)S(1)}, u32[]{:S(2)}, u32[]{:S(2)}) collective-permute-start(bf16[192,768]{1,0:T(8,128)(2,1)S(1)} %pad_maximum_fusion.4), channel_id=1, source_target_pairs={{2,0},{4,2},{6,4},{7,6},{5,7},{3,5},{1,3},{0,1},{10,8},{12,10},{14... | collective-permute-start | bytes 884744 | tf_op jit(solution)/shard_map/ppermute | solution.py:469
  861.0 27.4 %collective-permute-start.71 = (bf16[96,768]{1,0:T(8,128)(2,1)S(1)}, bf16[96,768]{1,0:T(8,128)(2,1)S(1)}, u32[]{:S(2)}, u32[]{:S(2)}) collective-permute-start(bf16[96,768]{1,0:T(8,128)(2,1)S(1)} %get-tuple-element.99), channel_id=1, source_target_pairs={{0,2},{2,4},{4,6},{6,7},{7,5},{5,3},{3,1},{1,0},{8,10},{10,12},{12... | collective-permute-start | bytes 442376 | tf_op jit(solution)/shard_map/ppermute | solution.py:466
  (143 other events, 2162.2 us)
